TPU v7x, 256 devices: a whole 4x4x8 slice. The times are simulated.
256 devices in a mesh: req: 8 (over x, core), ctx: 32 (over y, z).
Axes of the slice: x: 4, y: 4, z: 8, core: 2. Of those that a mesh axis runs over, the one named last changes fastest.
Arguments:
- context_q: bfloat16 [32768, 8192], P(('req', 'ctx')), parts along dimension 0, may hold values from -6 to 6, as said below
- context_key_value: bfloat16 [2, 32768, 1024], P(None, ('req', 'ctx')), parts along dimension 1, may hold values from -6 to 6, as said below
- query_token_queries: bfloat16 [1024, 8192], P(('req', 'ctx')), parts along dimension 0, may hold values from -6 to 6, as said below
- query_key_value: bfloat16 [2, 1024, 1024], P(None, ('req', 'ctx')), parts along dimension 1, may hold values from -6 to 6, as said below
Outputs:
- context_out: bfloat16 [32768, 8192], P(('req', 'ctx')), parts along dimension 0
- query_out: bfloat16 [1024, 8192], P(('req', 'ctx')), parts along dimension 0
There are 8 independent parts, one for each index of `req`. A program takes and returns all parts, laid end to end along the dimension named above; each array names one. Nothing has to cross between parts.
Inputs may be any that keep to these rules, and one draw needn't show every extreme that they name: `context_q`: attention queries after position encoding. `context_key_value`: keys after position encoding, and values. `query_token_queries`: attention queries after position encoding. `query_key_value`: keys after position encoding, and values.
All inputs are finite; a program needn't handle non-finite values.
Results may differ from a plain program's by a relative error of at most 0.0026.
Values may be sent and summed in bfloat16 or wider, within the bound.
No kernel may reach another device: no remote copies, remote signals or barrier semaphores. Data moves between devices by JAX's collectives and lax.ppermute only.
A program may use at most 320 MiB of HBM per device.

v0:
```python
import jax
import jax.numpy as jnp
from jax import lax
from jax.sharding import PartitionSpec as P

HEAD_FEATURES = 128


NEGATIVE_FILLER = -1e30


def from_root(value, axis, source):
    kept = jnp.where(lax.axis_index(axis) == source, value, 0).astype(value.dtype)
    return lax.psum(kept, axis)


def joined(part, axis, combine):
    gathered = jax.tree.map(lambda a: lax.all_gather(a, axis), part)

    def take(source):
        return jax.tree.map(lambda a: lax.dynamic_index_in_dim(a, source, 0, False), gathered)

    return lax.fori_loop(
        1, lax.axis_size(axis), lambda source, state: combine(state, take(source)), take(0)
    )


def attend_partial(query_matrix, key_row_list, value_row_list, allowed):
    scores = jnp.einsum(
        "rgjd,sgd->gjrs", query_matrix, key_row_list, preferred_element_type=jnp.float32
    ) * query_matrix.shape[-1] ** (-0.5)
    scores = jnp.where(allowed, scores, NEGATIVE_FILLER)
    maxima = jnp.max(scores, axis=-1, keepdims=True)
    weights = jnp.exp(scores - maxima)
    totals = jnp.sum(weights, axis=-1)
    outputs = jnp.einsum(
        "gjrs,sgd->rgjd",
        weights.astype(jnp.bfloat16),
        value_row_list,
        preferred_element_type=jnp.float32,
    )
    return (jnp.transpose(maxima[..., 0], (2, 0, 1)), jnp.transpose(totals, (2, 0, 1)), outputs)


def join_partials(first_part, second_part):
    highest = jnp.maximum(first_part[0], second_part[0])
    first_scale = jnp.exp(first_part[0] - highest)
    second_scale = jnp.exp(second_part[0] - highest)
    return (
        highest,
        first_part[1] * first_scale + second_part[1] * second_scale,
        first_part[2] * first_scale[..., None] + second_part[2] * second_scale[..., None],
    )


def per_device(context_q, context_key_value, query_token_queries, query_key_value):
    block_len = context_q.shape[0]
    head_dim = HEAD_FEATURES
    kv_heads = context_key_value.shape[2] // head_dim
    heads_per_group = context_q.shape[1] // context_key_value.shape[2]
    block_index = lax.axis_index("ctx")
    anchor = from_root(context_key_value, "ctx", 0)
    every_key = jnp.concatenate([anchor[0], context_key_value[0]], 0)
    every_value = jnp.concatenate([anchor[1], context_key_value[1]], 0)
    positions = jnp.arange(block_len)
    causal = positions[None, :] <= positions[:, None]
    anchor_ok = jnp.broadcast_to(block_index > 0, (block_len, block_len))
    allowed = jnp.concatenate([anchor_ok, causal], 1)

    def encode_head(head_index):
        query_matrix = lax.dynamic_slice_in_dim(
            context_q, head_index * heads_per_group * head_dim, heads_per_group * head_dim, 1
        )
        query_matrix = query_matrix.reshape(block_len, 1, heads_per_group, head_dim)
        key_portion = lax.dynamic_slice_in_dim(
            every_key, head_index * head_dim, head_dim, 1
        ).reshape(2 * block_len, 1, head_dim)
        value_portion = lax.dynamic_slice_in_dim(
            every_value, head_index * head_dim, head_dim, 1
        ).reshape(2 * block_len, 1, head_dim)
        maxima, totals, outputs = attend_partial(query_matrix, key_portion, value_portion, allowed)
        return (
            (outputs / totals[..., None])
            .astype(jnp.bfloat16)
            .reshape(block_len, heads_per_group * head_dim)
        )

    encoded = lax.map(encode_head, jnp.arange(kv_heads))
    context_out = jnp.transpose(encoded, (1, 0, 2)).reshape(
        block_len, kv_heads * heads_per_group * head_dim
    )
    gathered_q, gathered_kv = (
        lax.all_gather(query_token_queries, "ctx", axis=0, tiled=True),
        lax.all_gather(query_key_value, "ctx", axis=1, tiled=True),
    )
    query_total = gathered_q.shape[0]
    all_queries = gathered_q.reshape(query_total, kv_heads, heads_per_group, head_dim)
    block_keys = context_key_value[0].reshape(block_len, kv_heads, head_dim)
    block_values = context_key_value[1].reshape(block_len, kv_heads, head_dim)
    maxima, totals, outputs = attend_partial(all_queries, block_keys, block_values, True)
    own_rows = query_token_queries.shape[0]
    row_start = block_index * own_rows
    own_queries = query_token_queries.reshape(own_rows, kv_heads, heads_per_group, head_dim)
    key_pos = jnp.arange(query_total)
    row_pos = row_start + jnp.arange(own_rows)
    self_allowed = key_pos[None, :] <= row_pos[:, None]
    self_max, self_total, self_out = attend_partial(
        own_queries,
        gathered_kv[0].reshape(query_total, kv_heads, head_dim),
        gathered_kv[1].reshape(query_total, kv_heads, head_dim),
        self_allowed,
    )
    merged = joined((maxima, totals, outputs), "ctx", join_partials)
    row_max = lax.dynamic_slice_in_dim(merged[0], row_start, own_rows, 0)
    row_total = lax.dynamic_slice_in_dim(merged[1], row_start, own_rows, 0)
    row_out = lax.dynamic_slice_in_dim(merged[2], row_start, own_rows, 0)
    final_max = jnp.maximum(row_max, self_max)
    context_scale = jnp.exp(row_max - final_max)
    self_scale = jnp.exp(self_max - final_max)
    numerator = row_out * context_scale[..., None] + self_out * self_scale[..., None]
    denominator = row_total * context_scale + self_total * self_scale
    query_out = (numerator / denominator[..., None]).reshape(own_rows, -1).astype(jnp.bfloat16)
    return (context_out, query_out)


def solution(mesh):
    return jax.shard_map(
        per_device,
        mesh=mesh,
        in_specs=(
            P(("req", "ctx"), None),
            P(None, ("req", "ctx"), None),
            P(("req", "ctx"), None),
            P(None, ("req", "ctx"), None),
        ),
        out_specs=(P(("req", "ctx"), None), P(("req", "ctx"), None)),
        check_vma=False,
    )
```

profile of v0, /device:TPU:36, one launch (start us, length us, event | category | flops | bytes accessed | tf_op | source)
XLA Modules:
  0.0 1581.9 jit_solution(3388244745620368670)
XLA Ops:
  11.0 79.1 %all-gather.15.cloned.1.call-done = bf16[32,4,8192]{2,1,0:T(4,128)(2,1)} async-done(((bf16[1,4,8192]{2,1,0:T(4,128)(2,1)}), bf16[32,4,8192]{2,1,0:T(4,128)(2,1)}) %all-gather.15.cloned.1.call-update) | async-done | bytes 2097168 | tf_op jit(solution)/shard_map/all_gather | solution.py:93
  90.2 3.8 reshape.78
  100.1 5.2 convolution_bitcast_fusion.1
  106.0 48.1 %all_gather.31 = bf16[2,128,1024]{2,0,1:T(2,128)(2,1)S(1)} all-gather(bf16[2,4,1024]{2,0,1:T(2,128)(2,1)S(1)} %copy.68), channel_id=1, replica_groups=mesh['req'=8,'ctx'=32] {'ctx'}, dimensions={1}, use_global_device_ids=true | all-gather | bytes 540672 | tf_op jit(solution)/shard_map/all_gather | solution.py:94
  158.9 80.1 %all-reduce.3.cloned.1.call-done = bf16[2,128,1024]{1,2,0:T(8,128)(2,1)} async-done(((bf16[2,128,1024]{1,2,0:T(8,128)(2,1)}), bf16[2,128,1024]{1,2,0:T(8,128)(2,1)}) %all-reduce.3.cloned.1.call-update) | async-done | bytes 524304 | tf_op jit(solution)/shard_map/psum | solution.py:14
  241.9 39.7 %while.31 = (s32[]{:T(128)}, bf16[8,128,1024]{1,2,0:T(8,128)(2,1)S(1)}, s32[8]{0:T(128)S(1)}, bf16[256,1024]{0,1:T(8,128)(2,1)}, pred[128,256]{0,1:T(8,128)(4,1)...) while((s32[]{:T(128)}, ...), condition=%wide.region_4.5_spmd, body=%wide.region_1.4_spmd.sunk | while | flops 136312832 | bytes 5427445 | solution.py:88
  281.6 2.9 copy.83
  284.5 25.9 %all-gather.11.cloned.1.call-done = f32[4096,8,8]{0,2,1:T(8,128)} async-done(((f32[128,8,8]{0,2,1:T(8,128)}), f32[4096,8,8]{0,2,1:T(8,128)}) %all-gather.11.cloned.1.call-update) | async-done | bytes 1048592 | tf_op jit(solution)/shard_map/all_gather | solution.py:18
  311.9 71.8 %all-gather.9.cloned.1.call-done = f32[4096,8,8]{0,2,1:T(8,128)} async-done(((f32[128,8,8]{0,2,1:T(8,128)}), f32[4096,8,8]{0,2,1:T(8,128)}) %all-gather.9.cloned.1.call-update) | async-done | bytes 1048592 | tf_op jit(solution)/shard_map/all_gather | solution.py:18
  386.5 825.0 %all-gather.13.cloned.1.call-done = f32[4096,8,8,128]{3,0,2,1:T(8,128)} async-done(((f32[128,8,8,128]{3,0,2,1:T(8,128)}), f32[4096,8,8,128]{3,0,2,1:T(8,128)}) %all-gather.13.cloned.1.call-update) | async-done | bytes 134217744 | tf_op jit(solution)/shard_map/all_gather | solution.py:18
  1214.0 4.4 copy.62
  1218.4 354.5 %while.32 = (s32[]{:T(128)}, f32[128,8,8]{0,2,1:T(8,128)S(1)}, f32[128,8,8]{0,2,1:T(8,128)S(1)}, f32[128,8,8,128]{3,2,1,0:T(8,128)}, f32[32,128,8,8]{1,0,3,2:T(8...) while((s32[]{:T(128)}, f32[128,8,8]{0,2,1:T(8,128)S(1)}, ...), condition=%wide.region_8.9_spmd, body=%wide.region_7.8_spmd.sunk | while | flops 3194885 | bytes 55115980 | solution.py:23
  1219.0 2.6 constant_dynamic-slice_fusion.9
  1222.4 5.4 fusion.65
  1230.4 2.6 constant_dynamic-slice_fusion.9
  1233.9 5.4 fusion.65
  1241.9 2.6 constant_dynamic-slice_fusion.9
  1245.3 5.4 fusion.65
  1253.3 2.6 constant_dynamic-slice_fusion.9
  1256.8 5.4 fusion.65
  1264.7 2.6 constant_dynamic-slice_fusion.9
  1268.2 5.4 fusion.65
  1276.2 2.6 constant_dynamic-slice_fusion.9
  1279.6 5.4 fusion.65
  1287.6 2.6 constant_dynamic-slice_fusion.9
  1291.1 5.4 fusion.65
  1299.1 2.6 constant_dynamic-slice_fusion.9
  1302.5 5.4 fusion.65
  1310.5 2.6 constant_dynamic-slice_fusion.9
  1313.9 5.4 fusion.65
  1321.9 2.6 constant_dynamic-slice_fusion.9
  1325.4 5.4 fusion.65
  1333.4 2.6 constant_dynamic-slice_fusion.9
  1336.8 5.4 fusion.65
  1344.8 2.6 constant_dynamic-slice_fusion.9
  1348.2 5.4 fusion.65
  1356.2 2.6 constant_dynamic-slice_fusion.9
  1359.7 5.4 fusion.65
  1367.7 2.6 constant_dynamic-slice_fusion.9
  1371.1 5.4 fusion.65
  1379.1 2.6 constant_dynamic-slice_fusion.9
  1382.6 5.4 fusion.65
  1394.0 5.4 fusion.65
  1405.4 5.4 fusion.65
  1416.9 5.4 fusion.65
  1424.9 2.6 constant_dynamic-slice_fusion.9
  1428.3 5.4 fusion.65
  1436.3 2.6 constant_dynamic-slice_fusion.9
  1439.7 5.4 fusion.65
  1451.2 5.4 fusion.65
  1462.6 5.4 fusion.65
  1474.0 5.4 fusion.65
  1482.0 2.6 constant_dynamic-slice_fusion.9
  1485.5 5.4 fusion.65
  1493.5 2.6 constant_dynamic-slice_fusion.9
  1496.9 5.4 fusion.65
  1508.4 5.4 fusion.65
  1519.8 5.4 fusion.65
  1531.2 5.4 fusion.65
  1539.2 2.6 constant_dynamic-slice_fusion.9
  1542.7 5.4 fusion.65
  1550.7 2.6 constant_dynamic-slice_fusion.9
  1554.1 5.4 fusion.65
  1565.5 5.4 fusion.65
  (366 shorter events, 185.8 us)
Async XLA Ops:
  7.2 83.0 %all-gather.15.cloned.1.call-start = ((), (), s32[]{:S(2)}) async-start(), calls=%async_computation.4 | async-start | bytes 2162688 | tf_op jit(solution)/shard_map/all_gather | solution.py:93
  7.9 231.1 %all-reduce.3.cloned.1.call-start = ((), (), s32[]{:S(2)}) async-start(), calls=%async_computation | async-start | bytes 1048576 | tf_op jit(solution)/shard_map/psum | solution.py:14
  10.1 300.3 %all-gather.11.cloned.1.call-start = ((), (), s32[]{:S(2)}) async-start(), calls=%async_computation.2 | async-start | bytes 1081344 | tf_op jit(solution)/shard_map/all_gather | solution.py:18
  95.8 3.7 copy-start.3
  99.4 284.2 %all-gather.9.cloned.1.call-start = ((), (), s32[]{:S(2)}) async-start(), calls=%async_computation.1 | async-start | bytes 1081344 | tf_op jit(solution)/shard_map/all_gather | solution.py:18
  100.0 1111.5 %all-gather.13.cloned.1.call-start = ((), (), s32[]{:S(2)}) async-start(), calls=%async_computation.3 | async-start | bytes 138412032 | tf_op jit(solution)/shard_map/all_gather | solution.py:18
  105.2 51.7 %copy-start.6 = (bf16[4,8192]{1,0:T(4,128)(2,1)S(1)}, bf16[4,8192]{1,0:T(4,128)(2,1)}, u32[]{:S(2)}) copy-start(bf16[4,8192]{1,0:T(4,128)(2,1)} %param.10) | copy-start | bytes 196612
  1218.4 355.0 %copy-start.4 = (bf16[1,128,1024]{1,2,0:T(8,128)(2,1)S(1)}, bf16[1,128,1024]{1,2,0:T(8,128)(2,1)}, u32[]{:S(2)}) copy-start(bf16[1,128,1024]{1,2,0:T(8,128)(2,1)} %copy.98) | copy-start | bytes 786436
  1219.0 3.5 copy-start
  1227.9 2.0 copy-start.1
  1230.4 3.5 copy-start
  1239.3 2.0 copy-start.1
  1241.9 3.5 copy-start
  1250.7 2.0 copy-start.1
  1253.3 3.5 copy-start
  1262.2 2.0 copy-start.1
  1264.7 3.5 copy-start
  1273.6 2.0 copy-start.1
  1276.2 3.5 copy-start
  1285.0 2.0 copy-start.1
  1287.6 3.5 copy-start
  1296.5 2.0 copy-start.1
  1299.0 3.5 copy-start
  1307.9 2.0 copy-start.1
  1310.5 3.5 copy-start
  1319.4 2.0 copy-start.1
  1321.9 3.5 copy-start
  1330.8 2.0 copy-start.1
  1333.4 3.5 copy-start
  1342.2 2.0 copy-start.1
  1344.8 3.5 copy-start
  1353.7 2.0 copy-start.1
  1356.2 3.5 copy-start
  1365.1 2.0 copy-start.1
  1367.7 3.5 copy-start
  1376.5 2.0 copy-start.1
  1379.1 3.5 copy-start
  1388.0 2.0 copy-start.1
  1390.5 3.5 copy-start
  1399.4 2.0 copy-start.1
  1402.0 3.5 copy-start
  1413.4 3.5 copy-start
  1424.8 3.5 copy-start
  1433.7 2.0 copy-start.1
  1436.3 3.5 copy-start
  1445.2 2.0 copy-start.1
  1447.7 3.5 copy-start
  1456.6 2.0 copy-start.1
  1459.2 3.5 copy-start
  1470.6 3.5 copy-start
  1482.0 3.5 copy-start
  1490.9 2.0 copy-start.1
  1493.5 3.5 copy-start
  1502.3 2.0 copy-start.1
  1504.9 3.5 copy-start
  1513.8 2.0 copy-start.1
  1516.3 3.5 copy-start
  1527.8 3.5 copy-start
  1539.2 3.5 copy-start
  1548.1 2.0 copy-start.1
  1550.6 3.5 copy-start
  1559.5 2.0 copy-start.1
  1562.1 3.5 copy-start
  1570.9 2.0 copy-start.1
  (9 other events, 15.1 us)
Sparse Core Ops, SparseCore 0:
  10.6 79.5 all-gather.14
  94.1 144.7 all-reduce.2
  241.7 68.6 all-gather.10
  313.6 69.9 all-gather.8
  386.4 825.1 all-gather.12
where the time goes:
time: 1590 us; the launch traced here: 1580 us
  waiting for transfers between devices  1080 us (68%)
  local copies, waits for them, and re-layouts  227 us (14%)
  other arithmetic  175 us (11%)
  blocking collectives  48.1 us (3%)
  matrix products  21.6 us (1%)
    all_gather x3, waiting for transfers between devices, joined(): gathered = jax.tree.map(lambda a: lax.all_gather(a, axis), part)  923 us
    add x31, other arithmetic, join_partials(): first_part[2] * first_scale[..., None]  168 us
    dynamic_slice x65, local copies, waits for them, and re-layouts, take(): lax.dynamic_index_in_dim(a, source, 0, False)  87.7 us
    while x124, local copies, waits for them, and re-layouts  85.9 us
    psum x1, waiting for transfers between devices, from_root(): return lax.psum(kept, axis)  80.1 us
    all_gather x1, waiting for transfers between devices, per_device(): lax.all_gather(query_token_queries, 'ctx', axis=0, tiled=True)  79.1 us
    all_gather x1, blocking collectives, per_device(): lax.all_gather(query_key_value, 'ctx', axis=1, tiled=True)  48.1 us
  transfers between devices with their start and end apart: 5, of which 5 were waited for; matrix products, arithmetic and copies ran while one was open for 4% of the time, Pallas kernels for 0%

commit v1 on v0

v1 whole, which is shorter than its diff:
```python
import functools

import jax
import jax.numpy as jnp
from jax import lax
from jax.experimental import pallas as pl
from jax.experimental.pallas import tpu as pltpu
from jax.sharding import PartitionSpec as P

KV_HEADS = 8
GROUP = 8
D = 128
BLOCK = 128
QUARTERS = 4
CTX = QUARTERS * KV_HEADS
PIECE = BLOCK // QUARTERS
ROWS = 4
QROWS = ROWS * GROUP
F32 = jnp.float32
BF16 = jnp.bfloat16
FILLER = -1e30
LOG2E = 1.4426950408889634
SCALE = D ** -0.5 * LOG2E

A_K, A_V, A_Q, A_S = 0, PIECE, 2 * PIECE, 2 * PIECE + QROWS
A_ROWS = A_S + 8
B_HI, B_LO, B_K, B_V, B_S = 0, QROWS, 2 * QROWS, 2 * QROWS + PIECE, 2 * QROWS + 2 * PIECE
B_ROWS = B_S + 8


def dot_nt(a, b):
    return lax.dot_general(a, b, (((1,), (1,)), ((), ())), preferred_element_type=F32)


def dot_nn(a, b):
    return lax.dot_general(a, b, (((1,), (0,)), ((), ())), preferred_element_type=F32)


def pack_kernel(kv_ref, q_ref, qkv_ref, out_ref):
    q = q_ref[...].astype(F32)
    qkv = qkv_ref[...].astype(F32)
    for head in range(KV_HEADS):
        lanes = slice(head * D, (head + 1) * D)
        first = head * GROUP * D
        queries = jnp.concatenate(
            [q[:, first + j * D:first + (j + 1) * D] for j in range(GROUP)], 0
        ).astype(BF16)
        for quarter in range(QUARTERS):
            dest = quarter * KV_HEADS + head
            rows = slice(quarter * PIECE, (quarter + 1) * PIECE)
            out_ref[dest, A_K:A_K + PIECE, :] = kv_ref[0, rows, lanes]
            out_ref[dest, A_V:A_V + PIECE, :] = kv_ref[1, rows, lanes]
            out_ref[dest, A_Q:A_Q + QROWS, :] = queries
            out_ref[dest, A_S:A_ROWS, :] = jnp.concatenate(
                [qkv[0, quarter:quarter + 1, lanes], qkv[1, quarter:quarter + 1, lanes], jnp.zeros((6, D), F32)], 0
            ).astype(BF16)


CHUNK = 8


def query_kernel(place_ref, in_ref, out_ref):
    quarter = place_ref[0] // KV_HEADS
    keys = in_ref[:, A_K:A_K + PIECE, :].reshape(CTX * PIECE, D)
    values = in_ref[:, A_V:A_V + PIECE, :].reshape(CTX * PIECE, D)
    tail = in_ref[:, A_S:A_ROWS, :].astype(F32)
    self_keys = tail[:, 0, :].astype(BF16)
    self_values = tail[:, 1, :].astype(BF16)
    anchor = in_ref[0, A_K:A_V + PIECE, :]
    rows = CHUNK * QROWS
    row_id = lax.broadcasted_iota(jnp.int32, (rows, CTX), 0)
    key_pos = lax.broadcasted_iota(jnp.int32, (rows, CTX), 1) * ROWS + quarter
    row_pos = (row_id // QROWS) * ROWS + row_id % ROWS
    diagonal = (
        lax.broadcasted_iota(jnp.int32, (CHUNK, QROWS, D), 1)
        == lax.broadcasted_iota(jnp.int32, (CHUNK, QROWS, D), 2)
    )
    for chunk in range(CTX // CHUNK):
        sources = slice(chunk * CHUNK, (chunk + 1) * CHUNK)
        queries = in_ref[sources, A_Q:A_Q + QROWS, :].reshape(rows, D)
        scores = dot_nt(queries, keys)
        self_scores = dot_nt(queries, self_keys)
        self_scores = jnp.where(key_pos <= row_pos + chunk * CHUNK * ROWS, self_scores, FILLER)
        highest = jnp.maximum(jnp.max(scores, 1, keepdims=True), jnp.max(self_scores, 1, keepdims=True))
        weights = jnp.exp2((scores - highest) * SCALE)
        self_weights = jnp.exp2((self_scores - highest) * SCALE)
        total = jnp.sum(weights, 1, keepdims=True) + jnp.sum(self_weights, 1, keepdims=True)
        summed = dot_nn(weights.astype(BF16), values) + dot_nn(self_weights.astype(BF16), self_values)
        partial = (summed / total).reshape(CHUNK, QROWS, D)
        high = partial.astype(BF16)
        out_ref[sources, B_HI:B_HI + QROWS, :] = high
        out_ref[sources, B_LO:B_LO + QROWS, :] = (partial - high.astype(F32)).astype(BF16)
        log_sum = (highest * SCALE + jnp.log2(total)).reshape(CHUNK, QROWS, 1)
        log_row = jnp.sum(jnp.where(diagonal, log_sum, 0.0), 1, keepdims=True)
        first = log_row.astype(BF16).astype(F32)
        second = (log_row - first).astype(BF16).astype(F32)
        third = log_row - first - second
        out_ref[sources, B_S:B_ROWS, :] = jnp.concatenate(
            [first, second, third, jnp.zeros((CHUNK, 5, D), F32)], 1
        ).astype(BF16)
    out_ref[:, B_K:B_V + PIECE, :] = jnp.broadcast_to(anchor[None], (CTX, 2 * PIECE, D))


def encode_kernel(place_ref, q_ref, kv_ref, in_ref, out_ref, query_out_ref):
    head = pl.program_id(0)
    filler = jnp.where(place_ref[0] > 0, 0, BLOCK)
    anchor_keys = [in_ref[y * KV_HEADS + head, B_K:B_K + PIECE, :] for y in range(QUARTERS)]
    anchor_values = [in_ref[y * KV_HEADS + head, B_V:B_V + PIECE, :] for y in range(QUARTERS)]
    keys = jnp.concatenate(anchor_keys + [kv_ref[0]], 0)
    values = jnp.concatenate(anchor_values + [kv_ref[1]], 0)
    row = lax.broadcasted_iota(jnp.int32, (BLOCK, 2 * BLOCK), 0)
    column = lax.broadcasted_iota(jnp.int32, (BLOCK, 2 * BLOCK), 1)
    allowed = (column >= filler) & (column <= row + BLOCK)
    for j in range(GROUP):
        lanes = slice(j * D, (j + 1) * D)
        scores = jnp.where(allowed, dot_nt(q_ref[:, lanes], keys), FILLER)
        highest = jnp.max(scores, 1, keepdims=True)
        weights = jnp.exp2((scores - highest) * SCALE)
        total = jnp.sum(weights, 1, keepdims=True)
        out_ref[:, lanes] = (dot_nn(weights.astype(BF16), values) / total).astype(BF16)

    diagonal = (
        lax.broadcasted_iota(jnp.int32, (QROWS, D), 0) == lax.broadcasted_iota(jnp.int32, (QROWS, D), 1)
    )
    logs = []
    for y in range(QUARTERS):
        parts = in_ref[y * KV_HEADS + head, B_S:B_ROWS, :].astype(F32)
        logs.append(parts[0:1, :] + parts[1:2, :] + parts[2:3, :])
    highest = functools.reduce(jnp.maximum, logs)
    shares = [jnp.exp2(log - highest) for log in logs]
    whole = functools.reduce(jnp.add, shares)
    merged = jnp.zeros((QROWS, D), F32)
    for y in range(QUARTERS):
        share = jnp.sum(jnp.where(diagonal, shares[y] / whole, 0.0), 1, keepdims=True)
        partial = (
            in_ref[y * KV_HEADS + head, B_HI:B_HI + QROWS, :].astype(F32)
            + in_ref[y * KV_HEADS + head, B_LO:B_LO + QROWS, :].astype(F32)
        )
        merged = merged + share * partial
    for j in range(GROUP):
        query_out_ref[:, j * D:(j + 1) * D] = merged[j * ROWS:(j + 1) * ROWS, :].astype(BF16)


VMEM = pl.BlockSpec(memory_space=pltpu.VMEM)
SMEM = pl.BlockSpec(memory_space=pltpu.SMEM)
PARAMS = pltpu.CompilerParams(vmem_limit_bytes=40 * 1024 * 1024)


def per_device(context_q, context_key_value, query_token_queries, query_key_value):
    place = lax.axis_index("ctx").astype(jnp.int32).reshape(1)
    packed = pl.pallas_call(
        pack_kernel,
        out_shape=jax.ShapeDtypeStruct((CTX, A_ROWS, D), BF16),
        in_specs=[VMEM, VMEM, VMEM],
        out_specs=VMEM,
        compiler_params=PARAMS,
    )(context_key_value, query_token_queries, query_key_value)
    received = lax.all_to_all(packed, "ctx", 0, 0)
    partial = pl.pallas_call(
        query_kernel,
        out_shape=jax.ShapeDtypeStruct((CTX, B_ROWS, D), BF16),
        in_specs=[SMEM, VMEM],
        out_specs=VMEM,
        compiler_params=PARAMS,
    )(place, received)
    gathered = lax.all_to_all(partial, "ctx", 0, 0)
    width = GROUP * D
    return pl.pallas_call(
        encode_kernel,
        grid=(KV_HEADS,),
        out_shape=(
            jax.ShapeDtypeStruct(context_q.shape, BF16),
            jax.ShapeDtypeStruct(query_token_queries.shape, BF16),
        ),
        in_specs=[
            SMEM,
            pl.BlockSpec((BLOCK, width), lambda h: (0, h)),
            pl.BlockSpec((2, BLOCK, D), lambda h: (0, 0, h)),
            VMEM,
        ],
        out_specs=(
            pl.BlockSpec((BLOCK, width), lambda h: (0, h)),
            pl.BlockSpec((ROWS, width), lambda h: (0, h)),
        ),
        compiler_params=PARAMS,
    )(place, context_q, context_key_value, gathered)


def solution(mesh):
    return jax.shard_map(
        per_device,
        mesh=mesh,
        in_specs=(
            P(("req", "ctx"), None),
            P(None, ("req", "ctx"), None),
            P(("req", "ctx"), None),
            P(None, ("req", "ctx"), None),
        ),
        out_specs=(P(("req", "ctx"), None), P(("req", "ctx"), None)),
        check_vma=False,
    )
```

time: 1590 us -> 87 us (0.05)
  waiting for transfers between devices: 1080 us -> 24.5 us
  local copies, waits for them, and re-layouts: 227 us -> 2.6 us
  other arithmetic: 175 us -> 0 us
  matrix products: 21.6 us -> 0 us
    all_gather x4 -> x0, waiting for transfers between devices: 1000 us -> none  [the longest x3 923 us: joined(): gathered = jax.tree.map(lambda a: lax.all_gather(a, axis), part)]
    add x64 -> x0, other arithmetic: 169 us -> none  [the longest x31 168 us: join_partials(): first_part[2] * first_scale[..., None]]
    dynamic_slice x89 -> x0, local copies, waits for them, and re-layouts: 102 us -> none  [the longest x65 87.7 us: take(): lax.dynamic_index_in_dim(a, source, 0, False)]
    while x127 -> x0, local copies, waits for them, and re-layouts: 90.7 us -> none
    psum x1 -> x0, waiting for transfers between devices: 80.1 us -> none  [from_root(): return lax.psum(kept, axis)]
    all_gather x1 -> x0, blocking collectives: 48.1 us -> none  [per_device(): lax.all_gather(query_key_value, 'ctx', axis=1, tiled=True)]
    all_to_all x0 -> x1, blocking collectives: none -> 35.1 us  [per_device(): gathered = lax.all_to_all(partial, 'ctx', 0, 0)]
    all_to_all x0 -> x1, waiting for transfers between devices: none -> 24.5 us  [per_device(): received = lax.all_to_all(packed, 'ctx', 0, 0)]
  transfers between devices with their start and end apart: 5 -> 1, of which waited for: 5 -> 1; matrix products, arithmetic and copies ran while one was open for 4% -> 0% of each run, Pallas kernels for 0% -> 0%
where the time goes in v1:
time: 87 us; the launch traced here: 85.6 us
  blocking collectives  35.1 us (40%)
  waiting for transfers between devices  24.5 us (28%)
  Pallas kernels  11.4 us (13%)
  starting transfers between devices  11.4 us (13%)
  local copies, waits for them, and re-layouts  2.6 us (3%)
    all_to_all x1, blocking collectives, per_device(): gathered = lax.all_to_all(partial, 'ctx', 0, 0)  35.1 us
    all_to_all x1, waiting for transfers between devices, per_device(): received = lax.all_to_all(packed, 'ctx', 0, 0)  24.5 us
    all_to_all x1, starting transfers between devices, per_device(): received = lax.all_to_all(packed, 'ctx', 0, 0)  11.4 us
    pallas_call x1, Pallas kernels, per_device(): pl.pallas_call(encode_kernel, grid=(KV_HEADS,), out_shape=(jax.ShapeDtype...  7.85 us
    unnamed x10, local copies, waits for them, and re-layouts  2.6 us
    pallas_call x1, Pallas kernels, per_device(): pl.pallas_call(query_kernel, out_shape=jax.ShapeDtypeStruct((CTX, B_ROWS,...  2.51 us
  transfers between devices with their start and end apart: 1, of which 1 were waited for; matrix products, arithmetic and copies ran while one was open for 0% of the time, Pallas kernels for 0%

profile of v1, /device:TPU:36, one launch (start us, length us, event | category | flops | bytes accessed | tf_op | source)
XLA Modules:
  0.0 85.6 jit_solution(1488633372670510921)
XLA Ops:
  0.6 0.0 copy-start.1
  0.6 1.0 %copy-done.1 = bf16[2,128,1024]{2,1,0:T(8,128)(2,1)S(1)} copy-done((bf16[2,128,1024]{2,1,0:T(8,128)(2,1)S(1)}, bf16[2,128,1024]{2,1,0:T(8,128)(2,1)}, u32[]{:S(2)}) %copy-start.1) | copy-done | bytes 524312
  1.7 0.0 copy-start.3
  1.7 0.8 copy-done.3
  2.5 0.0 copy-start.4
  2.5 0.7 copy-done.4
  3.2 1.0 %shard_map.59 = bf16[32,104,128]{2,1,0:T(8,128)(2,1)} custom-call(bf16[2,128,1024]{2,1,0:T(8,128)(2,1)S(1)} %copy-done.1, bf16[4,8192]{1,0:T(4,128)(2,1)S(1)} %copy-done.3, bf16[2,4,1024]{2,1,0:T(4,128)(2,1)S(1)} %copy-done.4), custom_call_target="tpu_custom_call" | custom-call | tf_op jit(solution)/shard_map/pallas_call | solution.py:151
  4.3 11.4 %all-to-all-start = ((bf16[32,104,128]{2,1,0:T(8,128)(2,1)}), bf16[32,104,128]{2,1,0:T(8,128)(2,1)S(1)}, u32[]{:S(2)}, u32[]{:S(2)}) async-start(bf16[32,104,128]{2,1,0:T(8,128)(2,1)} %shard_map.59), calls=%async_computation | async-start | bytes 1703936 | tf_op jit(solution)/shard_map/all_to_all | solution.py:158
  15.6 24.5 %all-to-all-done.in_ref = bf16[32,104,128]{2,1,0:T(8,128)(2,1)S(1)} async-done(((bf16[32,104,128]{2,1,0:T(8,128)(2,1)}), bf16[32,104,128]{2,1,0:T(8,128)(2,1)S(1)}, u32[]{:S(2)}, u32[]{:S(2)}) %all-to-all-start) | async-done | bytes 852000 | tf_op jit(solution)/shard_map/all_to_all | solution.py:158
  40.1 0.0 copy-start
  40.2 0.0 copy-start.2
  40.2 2.5 %shard_map.60 = bf16[32,136,128]{2,1,0:T(8,128)(2,1)S(1)} custom-call(s32[1]{0:T(128)} %bitcast.place_ref, bf16[32,104,128]{2,1,0:T(8,128)(2,1)S(1)} %all-to-all-done.in_ref), custom_call_target="tpu_custom_call" | custom-call | tf_op jit(solution)/shard_map/pallas_call | solution.py:159
  42.7 35.1 %all_to_all.10.in_ref = bf16[32,136,128]{2,1,0:T(8,128)(2,1)S(1)} all-to-all(bf16[32,136,128]{2,1,0:T(8,128)(2,1)S(1)} %shard_map.60), channel_id=1, replica_groups=mesh['req'=8,'ctx'=32] {'ctx'}, dimensions={0} | all-to-all | bytes 2228224 | tf_op jit(solution)/shard_map/all_to_all | solution.py:166
  77.8 0.0 copy-done
  77.8 0.0 copy-done.2
  77.8 7.9 %shard_map.61 = (bf16[128,8192]{1,0:T(8,128)(2,1)}, bf16[4,8192]{1,0:T(4,128)(2,1)}) custom-call(s32[1]{0:T(128)} %bitcast.place_ref, bf16[128,8192]{1,0:T(8,128)(2,1)S(1)} %copy-done, bf16[2,128,1024]{2,1,0:T(8,128)(2,1)S(1)} %copy-done.2, bf16[32,136,128]{2,1,0:T(8,128)(2,1)S(1)} %all_to_all.10.in_ref), custom_call_target="tpu_custom_call" | custom-call | tf_op jit(solution)/shard_map/pallas_call | solution.py:168
Async XLA Ops:
  0.6 1.0 %copy-start.1 = (bf16[2,128,1024]{2,1,0:T(8,128)(2,1)S(1)}, bf16[2,128,1024]{2,1,0:T(8,128)(2,1)}, u32[]{:S(2)}) copy-start(bf16[2,128,1024]{2,1,0:T(8,128)(2,1)} %kv_ref.3) | copy-start | bytes 1572868
  1.7 0.8 copy-start.3
  2.5 0.7 copy-start.4
  4.3 35.9 %all-to-all-start = ((bf16[32,104,128]{2,1,0:T(8,128)(2,1)}), bf16[32,104,128]{2,1,0:T(8,128)(2,1)S(1)}, u32[]{:S(2)}, u32[]{:S(2)}) async-start(bf16[32,104,128]{2,1,0:T(8,128)(2,1)} %shard_map.59), calls=%async_computation | async-start | bytes 1703936 | tf_op jit(solution)/shard_map/all_to_all | solution.py:158
  40.1 37.6 %copy-start = (bf16[128,8192]{1,0:T(8,128)(2,1)S(1)}, bf16[128,8192]{1,0:T(8,128)(2,1)}, u32[]{:S(2)}) copy-start(bf16[128,8192]{1,0:T(8,128)(2,1)} %q_ref.3) | copy-start | bytes 6291460
  40.2 37.6 %copy-start.2 = (bf16[2,128,1024]{2,1,0:T(8,128)(2,1)S(1)}, bf16[2,128,1024]{2,1,0:T(8,128)(2,1)}, u32[]{:S(2)}) copy-start(bf16[2,128,1024]{2,1,0:T(8,128)(2,1)} %kv_ref.3) | copy-start | bytes 1572868

commit v2 on v1

v2 whole, which is shorter than its diff:
```python
import functools

import jax
import jax.numpy as jnp
from jax import lax
from jax.experimental import pallas as pl
from jax.experimental.pallas import tpu as pltpu
from jax.sharding import PartitionSpec as P

KV_HEADS = 8
GROUP = 8
D = 128
BLOCK = 128
QUARTERS = 4
CTX = QUARTERS * KV_HEADS
PIECE = BLOCK // QUARTERS
ROWS = 4
QROWS = ROWS * GROUP
F32 = jnp.float32
BF16 = jnp.bfloat16
FILLER = -1e30
LOG2E = 1.4426950408889634
SCALE = D ** -0.5 * LOG2E

A_K, A_V, A_Q, A_S = 0, PIECE, 2 * PIECE, 2 * PIECE + QROWS
A_ROWS = A_S + 8
B_S = QROWS
B_ROWS = B_S + 8


def dot_nt(a, b):
    return lax.dot_general(a, b, (((1,), (1,)), ((), ())), preferred_element_type=F32)


def dot_nn(a, b):
    return lax.dot_general(a, b, (((1,), (0,)), ((), ())), preferred_element_type=F32)


def pack_kernel(kv_hbm, q_hbm, qkv_hbm, out_ref, kv_ref, q_ref, qkv_ref, sems):
    copies = [
        pltpu.make_async_copy(source, target, sems.at[i])
        for i, (source, target) in enumerate(((q_hbm, q_ref), (qkv_hbm, qkv_ref), (kv_hbm, kv_ref)))
    ]
    for copy in copies:
        copy.start()
    for copy in copies:
        copy.wait()
    q = q_ref[...].astype(F32)
    qkv = qkv_ref[...].astype(F32)
    for head in range(KV_HEADS):
        lanes = slice(head * D, (head + 1) * D)
        first = head * GROUP * D
        queries = jnp.concatenate(
            [q[:, first + j * D:first + (j + 1) * D] for j in range(GROUP)], 0
        ).astype(BF16)
        for quarter in range(QUARTERS):
            dest = quarter * KV_HEADS + head
            rows = slice(quarter * PIECE, (quarter + 1) * PIECE)
            out_ref[dest, A_K:A_K + PIECE, :] = kv_ref[0, rows, lanes]
            out_ref[dest, A_V:A_V + PIECE, :] = kv_ref[1, rows, lanes]
            out_ref[dest, A_Q:A_Q + QROWS, :] = queries
            out_ref[dest, A_S:A_ROWS, :] = jnp.concatenate(
                [qkv[0, quarter:quarter + 1, lanes], qkv[1, quarter:quarter + 1, lanes], jnp.zeros((6, D), F32)], 0
            ).astype(BF16)


CHUNK = 8
STACK = 4


def query_kernel(place_ref, in_ref, out_ref):
    quarter = place_ref[0] // KV_HEADS
    keys = in_ref[:, A_K:A_K + PIECE, :].reshape(CTX * PIECE, D)
    values = in_ref[:, A_V:A_V + PIECE, :].reshape(CTX * PIECE, D)
    tail = in_ref[:, A_S:A_ROWS, :].astype(F32)
    self_keys = tail[:, 0, :].astype(BF16)
    self_values = tail[:, 1, :].astype(BF16)
    rows = CHUNK * QROWS
    row_id = lax.broadcasted_iota(jnp.int32, (rows, CTX), 0)
    key_pos = lax.broadcasted_iota(jnp.int32, (rows, CTX), 1) * ROWS + quarter
    row_pos = (row_id // QROWS) * ROWS + row_id % ROWS
    diagonal = (
        lax.broadcasted_iota(jnp.int32, (CHUNK, QROWS, D), 1)
        == lax.broadcasted_iota(jnp.int32, (CHUNK, QROWS, D), 2)
    )
    for chunk in range(CTX // CHUNK):
        sources = slice(chunk * CHUNK, (chunk + 1) * CHUNK)
        queries = in_ref[sources, A_Q:A_Q + QROWS, :].reshape(rows, D)
        scores = dot_nt(queries, keys)
        self_scores = dot_nt(queries, self_keys)
        self_scores = jnp.where(key_pos <= row_pos + chunk * CHUNK * ROWS, self_scores, FILLER)
        highest = jnp.maximum(jnp.max(scores, 1, keepdims=True), jnp.max(self_scores, 1, keepdims=True))
        weights = jnp.exp2((scores - highest) * SCALE)
        self_weights = jnp.exp2((self_scores - highest) * SCALE)
        total = jnp.sum(weights, 1, keepdims=True) + jnp.sum(self_weights, 1, keepdims=True)
        summed = dot_nn(weights.astype(BF16), values) + dot_nn(self_weights.astype(BF16), self_values)
        partial = (summed / total).reshape(CHUNK, QROWS, D)
        out_ref[sources, 0:QROWS, :] = partial
        log_sum = (highest * SCALE + jnp.log2(total)).reshape(CHUNK, QROWS, 1)
        log_row = jnp.sum(jnp.where(diagonal, log_sum, 0.0), 1, keepdims=True)
        first = log_row.astype(BF16).astype(F32)
        second = (log_row - first).astype(BF16).astype(F32)
        third = log_row - first - second
        out_ref[sources, B_S:B_ROWS, :] = jnp.concatenate(
            [first, second, third, jnp.zeros((CHUNK, 5, D), F32)], 1
        )


def encode_kernel(
    place_ref, q_hbm, kv_hbm, a0_hbm, a1_hbm, a2_hbm, a3_hbm, out_hbm, q_ref, kv_ref, out_ref, q_sems, kv_sems, sems
):
    width = GROUP * D

    def copy_in(head):
        lanes = pl.ds(pl.multiple_of(head * width, width), width)
        return pltpu.make_async_copy(q_hbm.at[:, lanes], q_ref.at[:, lanes], q_sems.at[head])

    def copy_out(head):
        lanes = pl.ds(pl.multiple_of(head * width, width), width)
        return pltpu.make_async_copy(out_ref.at[:, lanes], out_hbm.at[:, lanes], sems.at[head])

    copies = [
        pltpu.make_async_copy(source, kv_ref.at[:, PIECE * i:PIECE * i + source.shape[1], :], kv_sems.at[i])
        for i, source in enumerate((a0_hbm, a1_hbm, a2_hbm, a3_hbm, kv_hbm))
    ]
    for copy in copies:
        copy.start()
    for head in range(KV_HEADS):
        copy_in(head).start()
    filler = jnp.where(place_ref[0] > 0, 0, BLOCK)
    row = lax.broadcasted_iota(jnp.int32, (BLOCK, 2 * BLOCK), 0)
    column = lax.broadcasted_iota(jnp.int32, (BLOCK, 2 * BLOCK), 1)
    allowed = (column >= filler) & (column <= row + BLOCK)
    for copy in copies:
        copy.wait()

    def one_head(head, carry):
        copy_in(head).wait()
        kv_lanes = pl.ds(pl.multiple_of(head * D, D), D)
        keys = kv_ref[0, :, kv_lanes]
        values = kv_ref[1, :, kv_lanes]
        for first in range(0, GROUP, STACK):
            lanes = [pl.ds(pl.multiple_of(head * width + (first + j) * D, D), D) for j in range(STACK)]
            queries = jnp.concatenate([q_ref[:, each] for each in lanes], 0)
            scores = dot_nt(queries, keys).reshape(STACK, BLOCK, 2 * BLOCK)
            scores = jnp.where(allowed[None], scores, FILLER)
            highest = jnp.max(scores, 2, keepdims=True)
            weights = jnp.exp2((scores - highest) * SCALE)
            total = jnp.sum(weights, 2, keepdims=True)
            summed = dot_nn(weights.astype(BF16).reshape(STACK * BLOCK, 2 * BLOCK), values)
            attended = (summed.reshape(STACK, BLOCK, D) / total).astype(BF16)
            for j in range(STACK):
                out_ref[:, lanes[j]] = attended[j]
        copy_out(head).start()
        return carry

    lax.fori_loop(0, KV_HEADS, one_head, 0)
    for head in range(KV_HEADS):
        copy_out(head).wait()


def merge_kernel(in_ref, out_ref):
    diagonal = (
        lax.broadcasted_iota(jnp.int32, (KV_HEADS, QROWS, D), 1)
        == lax.broadcasted_iota(jnp.int32, (KV_HEADS, QROWS, D), 2)
    )
    logs = []
    for y in range(QUARTERS):
        parts = in_ref[y * KV_HEADS:(y + 1) * KV_HEADS, B_S:B_ROWS, :]
        logs.append(parts[:, 0:1, :] + parts[:, 1:2, :] + parts[:, 2:3, :])
    highest = functools.reduce(jnp.maximum, logs)
    shares = [jnp.exp2(log - highest) for log in logs]
    whole = functools.reduce(jnp.add, shares)
    merged = jnp.zeros((KV_HEADS, QROWS, D), F32)
    for y in range(QUARTERS):
        share = jnp.sum(jnp.where(diagonal, shares[y] / whole, 0.0), 2, keepdims=True)
        sources = slice(y * KV_HEADS, (y + 1) * KV_HEADS)
        merged = merged + share * in_ref[sources, 0:QROWS, :]
    for head in range(KV_HEADS):
        for j in range(GROUP):
            first = (head * GROUP + j) * D
            out_ref[:, first:first + D] = merged[head, j * ROWS:(j + 1) * ROWS, :].astype(BF16)


VMEM = pl.BlockSpec(memory_space=pltpu.VMEM)
ANY = pl.BlockSpec(memory_space=pl.ANY)
SMEM = pl.BlockSpec(memory_space=pltpu.SMEM)
HBM = pl.BlockSpec(memory_space=pltpu.HBM)
PARAMS = pltpu.CompilerParams(vmem_limit_bytes=32 * 1024 * 1024)


def cost(flops, nbytes):
    return pl.CostEstimate(flops=flops, bytes_accessed=nbytes, transcendentals=0)


def at(quarter, z):
    return quarter * KV_HEADS + z


def scatter_anchor(kv):
    quarters = [kv[:, q * PIECE:(q + 1) * PIECE, :] for q in range(QUARTERS)]
    mine = jnp.where(lax.axis_index("ctx") == 0, quarters[0], 0)
    for q in range(1, QUARTERS):
        mine = mine + lax.ppermute(quarters[q], "ctx", [(0, at(q, 0))])
    return mine


def fan_along_z(mine):
    root = mine
    for step in (4, 2, 6):
        mine = mine + lax.ppermute(root, "ctx", [(at(y, 0), at(y, step)) for y in range(QUARTERS)])
    return mine


def pair_along_z(mine):
    pairs = [(at(y, z), at(y, z + 1)) for y in range(QUARTERS) for z in range(0, KV_HEADS, 2)]
    return mine + lax.ppermute(mine, "ctx", pairs)


def gather_along_y(mine):
    devices = [(y, z) for y in range(QUARTERS) for z in range(KV_HEADS)]
    return [mine] + [
        lax.ppermute(mine, "ctx", [(at(y, z), at((y + k) % QUARTERS, z)) for y, z in devices])
        for k in range(1, QUARTERS)
    ]


def per_device(context_q, context_key_value, query_token_queries, query_key_value):
    place = lax.axis_index("ctx").astype(jnp.int32).reshape(1)
    packed = pl.pallas_call(
        pack_kernel,
        out_shape=jax.ShapeDtypeStruct((CTX, A_ROWS, D), BF16),
        in_specs=[HBM, HBM, HBM],
        out_specs=VMEM,
        scratch_shapes=[
            pltpu.VMEM(context_key_value.shape, BF16),
            pltpu.VMEM(query_token_queries.shape, BF16),
            pltpu.VMEM(query_key_value.shape, BF16),
            pltpu.SemaphoreType.DMA((3,)),
        ],
        compiler_params=pltpu.CompilerParams(vmem_limit_bytes=60 * 1024 * 1024),
        cost_estimate=cost(0, 1 << 21),
    )(context_key_value, query_token_queries, query_key_value)
    quarter = scatter_anchor(context_key_value)
    received = lax.all_to_all(packed, "ctx", 0, 0)
    quarter = fan_along_z(quarter)
    received, quarter = lax.optimization_barrier((received, quarter))
    quarter = pair_along_z(quarter)
    partial = pl.pallas_call(
        query_kernel,
        out_shape=jax.ShapeDtypeStruct((CTX, B_ROWS, D), F32),
        in_specs=[SMEM, VMEM],
        out_specs=VMEM,
        compiler_params=PARAMS,
        cost_estimate=cost(1 << 29, 1 << 21),
    )(place, received)
    partial, quarter = lax.optimization_barrier((partial, quarter))
    anchor = gather_along_y(quarter)
    gathered = lax.all_to_all(partial.astype(jnp.float16), "ctx", 0, 0).astype(F32)
    context_out = pl.pallas_call(
        encode_kernel,
        out_shape=jax.ShapeDtypeStruct(context_q.shape, BF16),
        in_specs=[SMEM, HBM, HBM] + [ANY] * QUARTERS,
        out_specs=HBM,
        scratch_shapes=[
            pltpu.VMEM(context_q.shape, BF16),
            pltpu.VMEM((2, 2 * BLOCK, KV_HEADS * D), BF16),
            pltpu.VMEM(context_q.shape, BF16),
            pltpu.SemaphoreType.DMA((KV_HEADS,)),
            pltpu.SemaphoreType.DMA((QUARTERS + 1,)),
            pltpu.SemaphoreType.DMA((KV_HEADS,)),
        ],
        compiler_params=pltpu.CompilerParams(vmem_limit_bytes=56 * 1024 * 1024),
        cost_estimate=cost(1 << 36, 1 << 24),
    )(place, context_q, context_key_value, *anchor)
    query_out = pl.pallas_call(
        merge_kernel,
        out_shape=jax.ShapeDtypeStruct(query_token_queries.shape, BF16),
        in_specs=[VMEM],
        out_specs=VMEM,
        compiler_params=PARAMS,
        cost_estimate=cost(1 << 20, 1 << 20),
    )(gathered)
    return context_out, query_out


def solution(mesh):
    return jax.shard_map(
        per_device,
        mesh=mesh,
        in_specs=(
            P(("req", "ctx"), None),
            P(None, ("req", "ctx"), None),
            P(("req", "ctx"), None),
            P(None, ("req", "ctx"), None),
        ),
        out_specs=(P(("req", "ctx"), None), P(("req", "ctx"), None)),
        check_vma=False,
    )
```

time: 87 us -> 71.5 us (0.82); the launches traced: 85.6 us -> 71 us
  blocking collectives: 35.1 us -> 0 us
  starting transfers between devices: 11.4 us -> 27.9 us
  waiting for transfers between devices: 24.5 us -> 26.7 us
  Pallas kernels: 11.4 us -> 13.3 us
  local copies, waits for them, and re-layouts: 2.6 us -> 1.34 us
  other arithmetic: 0 us -> 0.91 us
    all_to_all x1 -> x0, blocking collectives: 35.1 us -> none  [per_device(): gathered = lax.all_to_all(partial, 'ctx', 0, 0)]
    ppermute x0 -> x10, starting transfers between devices: none -> 8.3 us  [the longest x3 3.01 us: gather_along_y(): lax.ppermute(mine, 'ctx', [(at(y, z), at((y + k) % QUARTERS, z)) for y, z...]
    all_to_all x0 -> x1, starting transfers between devices: none -> 8.19 us  [per_device(): lax.all_to_all(partial.astype(jnp.float16), 'ctx', 0, 0).astype(F32)]
    all_to_all x1, waiting for transfers between devices: 24.5 us -> 20.8 us  [per_device(): received = lax.all_to_all(packed, 'ctx', 0, 0)]
    ppermute x0 -> x10, waiting for transfers between devices: none -> 3.14 us  [the longest x1 3.12 us: pair_along_z(): return mine + lax.ppermute(mine, 'ctx', pairs)]
    all_to_all x0 -> x1, waiting for transfers between devices: none -> 2.77 us  [per_device(): lax.all_to_all(partial.astype(jnp.float16), 'ctx', 0, 0).astype(F32)]
    unnamed x10, local copies, waits for them, and re-layouts: 2.6 us -> 1.31 us
    pallas_call x1, Pallas kernels: 1.04 us -> 2.21 us  [per_device(): pl.pallas_call(pack_kernel, out_shape=jax.ShapeDtypeStruct((CTX, A_ROWS,...]
  transfers between devices with their start and end apart: 1 -> 12, of which waited for: 1 -> 3; matrix products, arithmetic and copies ran while one was open for 0% -> 1% of each run, Pallas kernels for 0% -> 14%
where the time goes in v2:
time: 71.5 us; the launch traced here: 71 us
  starting transfers between devices  27.9 us (39%)
  waiting for transfers between devices  26.7 us (37%)
  Pallas kernels  13.3 us (19%)
  local copies, waits for them, and re-layouts  1.34 us (2%)
  other arithmetic  0.91 us (1%)
  between operations  0.89 us (1%)
    all_to_all x1, waiting for transfers between devices, per_device(): received = lax.all_to_all(packed, 'ctx', 0, 0)  20.8 us
    all_to_all x1, starting transfers between devices, per_device(): received = lax.all_to_all(packed, 'ctx', 0, 0)  11.4 us
    all_to_all x1, starting transfers between devices, per_device(): lax.all_to_all(partial.astype(jnp.float16), 'ctx', 0, 0).astype(F32)  8.19 us
    pallas_call x1, Pallas kernels, per_device(): pl.pallas_call(encode_kernel, out_shape=jax.ShapeDtypeStruct(context_q.sh...  7.77 us
    ppermute x1, waiting for transfers between devices, pair_along_z(): return mine + lax.ppermute(mine, 'ctx', pairs)  3.12 us
    ppermute x3, starting transfers between devices, gather_along_y(): lax.ppermute(mine, 'ctx', [(at(y, z), at((y + k) % QUARTERS, z)) for y, z...  3.01 us
    all_to_all x1, waiting for transfers between devices, per_device(): lax.all_to_all(partial.astype(jnp.float16), 'ctx', 0, 0).astype(F32)  2.77 us
    pallas_call x1, Pallas kernels, per_device(): pl.pallas_call(query_kernel, out_shape=jax.ShapeDtypeStruct((CTX, B_ROWS,...  2.43 us
  transfers between devices with their start and end apart: 12, of which 3 were waited for; matrix products, arithmetic and copies ran while one was open for 1% of the time, Pallas kernels for 14%

profile of v2, /device:TPU:36, one launch (start us, length us, event | category | flops | bytes accessed | tf_op | source)
XLA Modules:
  0.0 71.0 jit_solution(660751109268932453)
XLA Ops:
  0.6 0.0 copy-start
  0.6 2.2 %shard_map.59 = bf16[32,104,128]{2,1,0:T(8,128)(2,1)} custom-call(bf16[2,128,1024]{2,1,0:T(8,128)(2,1)} %kv_hbm.3, bf16[4,8192]{1,0:T(4,128)(2,1)} %q_hbm.2, bf16[2,4,1024]{2,1,0:T(4,128)(2,1)} %qkv_hbm.1), custom_call_target="tpu_custom_call" | custom-call | bytes 2097152 | tf_op jit(solution)/shard_map/pallas_call | solution.py:230
  2.9 11.4 %all-to-all-start = ((bf16[32,104,128]{2,1,0:T(8,128)(2,1)}), bf16[32,104,128]{2,1,0:T(8,128)(2,1)S(1)}, u32[]{:S(2)}, u32[]{:S(2)}) async-start(bf16[32,104,128]{2,1,0:T(8,128)(2,1)} %shard_map.59), calls=%async_computation | async-start | bytes 1703936 | tf_op jit(solution)/shard_map/all_to_all | solution.py:245
  14.2 0.0 copy-done
  14.3 0.7 collective-permute-start
  15.0 0.7 collective-permute-start.1
  15.6 0.7 collective-permute-start.2
  16.3 0.0 collective-permute-done
  16.3 0.0 collective-permute-done.1
  16.3 0.0 collective-permute-done.2
  16.4 0.7 collective-permute-start.5
  17.1 0.7 collective-permute-start.4
  17.7 0.7 collective-permute-start.3
  18.4 0.0 collective-permute-done.5
  18.4 0.0 collective-permute-done.4
  18.4 0.0 collective-permute-done.3
  18.5 20.8 %all-to-all-done.in_ref = bf16[32,104,128]{2,1,0:T(8,128)(2,1)S(1)} async-done(((bf16[32,104,128]{2,1,0:T(8,128)(2,1)}), bf16[32,104,128]{2,1,0:T(8,128)(2,1)S(1)}, u32[]{:S(2)}, u32[]{:S(2)}) %all-to-all-start) | async-done | bytes 852000 | tf_op jit(solution)/shard_map/all_to_all | solution.py:245
  39.3 1.3 %collective-permute-start.6 = (bf16[2,32,1024]{2,1,0:T(8,128)(2,1)S(1)}, bf16[2,32,1024]{2,1,0:T(8,128)(2,1)S(1)}, u32[]{:S(2)}, u32[]{:S(2)}) collective-permute-start(bf16[2,32,1024]{2,1,0:T(8,128)(2,1)S(1)} %add_add_fusion), channel_id=1, source_target_pairs={{0,1},{2,3},{4,5},{6,7},{8,9},{10,11},{12,13},{14,15},{16,17},{18,... | collective-permute-start | bytes 393224 | tf_op jit(solution)/shard_map/ppermute | solution.py:217
  40.6 2.4 %shard_map.60 = f32[32,40,128]{2,1,0:T(8,128)S(1)} custom-call(s32[1]{0:T(128)} %bitcast.place_ref, bf16[32,104,128]{2,1,0:T(8,128)(2,1)S(1)} %all-to-all-done.in_ref), custom_call_target="tpu_custom_call" | custom-call | flops 536870912 | bytes 2097152 | tf_op jit(solution)/shard_map/pallas_call | solution.py:249
  43.1 3.1 %collective-permute-done.6 = bf16[2,32,1024]{2,1,0:T(8,128)(2,1)S(1)} collective-permute-done((bf16[2,32,1024]{2,1,0:T(8,128)(2,1)S(1)}, bf16[2,32,1024]{2,1,0:T(8,128)(2,1)S(1)}, u32[]{:S(2)}, u32[]{:S(2)}) %collective-permute-start.6) | collective-permute-done | bytes 131104 | tf_op jit(solution)/shard_map/ppermute | solution.py:217
  46.2 0.0 copy-start.1
  46.2 1.2 %collective-permute-start.9 = (bf16[2,32,1024]{2,1,0:T(8,128)(2,1)S(1)}, bf16[2,32,1024]{2,1,0:T(8,128)(2,1)S(1)}, u32[]{:S(2)}, u32[]{:S(2)}) collective-permute-start(bf16[2,32,1024]{2,1,0:T(8,128)(2,1)S(1)} %add.27.a0_hbm), channel_id=1, source_target_pairs={{0,24},{1,25},{2,26},{3,27},{4,28},{5,29},{6,30},{7,31},{8,0},{9,1... | collective-permute-start | bytes 393224 | tf_op jit(solution)/shard_map/ppermute | solution.py:223
  47.5 1.5 %collective-permute-start.8 = (bf16[2,32,1024]{2,1,0:T(8,128)(2,1)S(1)}, bf16[2,32,1024]{2,1,0:T(8,128)(2,1)S(1)}, u32[]{:S(2)}, u32[]{:S(2)}) collective-permute-start(bf16[2,32,1024]{2,1,0:T(8,128)(2,1)S(1)} %add.27.a0_hbm), channel_id=1, source_target_pairs={{0,16},{1,17},{2,18},{3,19},{4,20},{5,21},{6,22},{7,23},{8,24},{9,... | collective-permute-start | bytes 393224 | tf_op jit(solution)/shard_map/ppermute | solution.py:223
  49.0 0.2 collective-permute-start.7
  49.2 0.8 %convert_element_type.8 = f16[32,40,128]{2,1,0:T(8,128)(2,1)} convert(f32[32,40,128]{2,1,0:T(8,128)S(1)} %shard_map.60) | non-fusion elementwise | flops 163840 | bytes 983040 | tf_op jit(solution)/shard_map/convert_element_type | solution.py:259
  50.0 8.2 %all-to-all-start.1 = ((f16[32,40,128]{2,1,0:T(8,128)(2,1)}), f16[32,40,128]{2,1,0:T(8,128)(2,1)S(1)}, u32[]{:S(2)}, u32[]{:S(2)}) async-start(f16[32,40,128]{2,1,0:T(8,128)(2,1)} %convert_element_type.8), calls=%async_computation.1 | async-start | bytes 655360 | tf_op jit(solution)/shard_map/all_to_all | solution.py:259
  58.2 0.0 collective-permute-done.9.a3_hbm
  58.2 0.0 copy-start.2
  58.2 0.0 collective-permute-done.8.a2_hbm
  58.2 0.0 copy-start.3
  58.2 0.0 collective-permute-done.7.a1_hbm
  58.3 0.0 copy-done.1
  58.3 0.6 copy-done.2
  58.9 0.1 copy-done.3
  58.9 0.0 copy-start.4
  58.9 0.6 copy-done.4
  59.6 7.8 %shard_map.61 = bf16[128,8192]{1,0:T(8,128)(2,1)} custom-call(s32[1]{0:T(128)} %bitcast.place_ref, bf16[128,8192]{1,0:T(8,128)(2,1)} %q_hbm.3, bf16[2,128,1024]{2,1,0:T(8,128)(2,1)} %kv_hbm.3, bf16[2,32,1024]{2,1,0:T(8,128)(2,1)} %copy-done.1, bf16[2,32,1024]{2,1,0:T(8,128)(2,1)} %copy-done.4, bf16[2,32,1024]{2,1,0:T(8,128)(2,1)} %copy-done.3, ...), custom_call_target="tpu_custom_call" | custom-call | flops 68719476736 | bytes 16777216 | tf_op jit(solution)/shard_map/pallas_call | solution.py:260
  67.3 2.8 %all-to-all-done.1 = f16[32,40,128]{2,1,0:T(8,128)(2,1)S(1)} async-done(((f16[32,40,128]{2,1,0:T(8,128)(2,1)}), f16[32,40,128]{2,1,0:T(8,128)(2,1)S(1)}, u32[]{:S(2)}, u32[]{:S(2)}) %all-to-all-start.1) | async-done | bytes 327712 | tf_op jit(solution)/shard_map/all_to_all | solution.py:259
  70.2 0.9 %shard_map.62 = bf16[4,8192]{1,0:T(4,128)(2,1)} custom-call(f32[32,40,128]{2,1,0:T(8,128)S(1)} %convert_element_type.9.in_ref), custom_call_target="tpu_custom_call" | custom-call | flops 1048576 | bytes 1048576 | tf_op jit(solution)/shard_map/pallas_call | solution.py:276
  (5 shorter events, 0.2 us)
Async XLA Ops:
  0.6 13.6 %copy-start = (bf16[2,128,1024]{2,1,0:T(8,128)(2,1)S(1)}, bf16[2,128,1024]{2,1,0:T(8,128)(2,1)}, u32[]{:S(2)}) copy-start(bf16[2,128,1024]{2,1,0:T(8,128)(2,1)} %kv_hbm.3) | copy-start | bytes 1572868
  2.9 36.5 %all-to-all-start = ((bf16[32,104,128]{2,1,0:T(8,128)(2,1)}), bf16[32,104,128]{2,1,0:T(8,128)(2,1)S(1)}, u32[]{:S(2)}, u32[]{:S(2)}) async-start(bf16[32,104,128]{2,1,0:T(8,128)(2,1)} %shard_map.59), calls=%async_computation | async-start | bytes 1703936 | tf_op jit(solution)/shard_map/all_to_all | solution.py:245
  14.3 2.0 %collective-permute-start = (bf16[2,32,1024]{2,1,0:T(8,128)(2,1)S(1)}, bf16[2,32,1024]{2,1,0:T(8,128)(2,1)S(1)}, u32[]{:S(2)}, u32[]{:S(2)}) collective-permute-start(bf16[2,32,1024]{2,1,0:T(8,128)(2,1)S(1)} %get-tuple-element.10), channel_id=1, source_target_pairs={{0,8},{32,40},{64,72},{96,104},{128,136},{160,168},{192,200},{224,... | collective-permute-start | bytes 393224 | tf_op jit(solution)/shard_map/ppermute | solution.py:204
  15.0 1.4 %collective-permute-start.1 = (bf16[2,32,1024]{2,1,0:T(8,128)(2,1)S(1)}, bf16[2,32,1024]{2,1,0:T(8,128)(2,1)S(1)}, u32[]{:S(2)}, u32[]{:S(2)}) collective-permute-start(bf16[2,32,1024]{2,1,0:T(8,128)(2,1)S(1)} %get-tuple-element.11), channel_id=1, source_target_pairs={{0,16},{32,48},{64,80},{96,112},{128,144},{160,176},{192,208},{224... | collective-permute-start | bytes 393224 | tf_op jit(solution)/shard_map/ppermute | solution.py:204
  15.6 0.7 collective-permute-start.2
  16.4 2.0 %collective-permute-start.5 = (bf16[2,32,1024]{2,1,0:T(8,128)(2,1)S(1)}, bf16[2,32,1024]{2,1,0:T(8,128)(2,1)S(1)}, u32[]{:S(2)}, u32[]{:S(2)}) collective-permute-start(bf16[2,32,1024]{2,1,0:T(8,128)(2,1)S(1)} %add_add_fusion.1), channel_id=1, source_target_pairs={{0,6},{8,14},{16,22},{24,30},{32,38},{40,46},{48,54},{56,62},{64,7... | collective-permute-start | bytes 393224 | tf_op jit(solution)/shard_map/ppermute | solution.py:211
  17.1 1.4 %collective-permute-start.4 = (bf16[2,32,1024]{2,1,0:T(8,128)(2,1)S(1)}, bf16[2,32,1024]{2,1,0:T(8,128)(2,1)S(1)}, u32[]{:S(2)}, u32[]{:S(2)}) collective-permute-start(bf16[2,32,1024]{2,1,0:T(8,128)(2,1)S(1)} %add_add_fusion.1), channel_id=1, source_target_pairs={{0,2},{8,10},{16,18},{24,26},{32,34},{40,42},{48,50},{56,58},{64,6... | collective-permute-start | bytes 393224 | tf_op jit(solution)/shard_map/ppermute | solution.py:211
  17.7 0.7 collective-permute-start.3
  39.3 6.8 %collective-permute-start.6 = (bf16[2,32,1024]{2,1,0:T(8,128)(2,1)S(1)}, bf16[2,32,1024]{2,1,0:T(8,128)(2,1)S(1)}, u32[]{:S(2)}, u32[]{:S(2)}) collective-permute-start(bf16[2,32,1024]{2,1,0:T(8,128)(2,1)S(1)} %add_add_fusion), channel_id=1, source_target_pairs={{0,1},{2,3},{4,5},{6,7},{8,9},{10,11},{12,13},{14,15},{16,17},{18,... | collective-permute-start | bytes 393224 | tf_op jit(solution)/shard_map/ppermute | solution.py:217
  46.2 12.0 %copy-start.1 = (bf16[2,32,1024]{2,1,0:T(8,128)(2,1)}, bf16[2,32,1024]{2,1,0:T(8,128)(2,1)S(1)}, u32[]{:S(2)}) copy-start(bf16[2,32,1024]{2,1,0:T(8,128)(2,1)S(1)} %add.27.a0_hbm) | copy-start | bytes 393220
  46.2 12.0 %collective-permute-start.9 = (bf16[2,32,1024]{2,1,0:T(8,128)(2,1)S(1)}, bf16[2,32,1024]{2,1,0:T(8,128)(2,1)S(1)}, u32[]{:S(2)}, u32[]{:S(2)}) collective-permute-start(bf16[2,32,1024]{2,1,0:T(8,128)(2,1)S(1)} %add.27.a0_hbm), channel_id=1, source_target_pairs={{0,24},{1,25},{2,26},{3,27},{4,28},{5,29},{6,30},{7,31},{8,0},{9,1... | collective-permute-start | bytes 393224 | tf_op jit(solution)/shard_map/ppermute | solution.py:223
  47.5 10.8 %collective-permute-start.8 = (bf16[2,32,1024]{2,1,0:T(8,128)(2,1)S(1)}, bf16[2,32,1024]{2,1,0:T(8,128)(2,1)S(1)}, u32[]{:S(2)}, u32[]{:S(2)}) collective-permute-start(bf16[2,32,1024]{2,1,0:T(8,128)(2,1)S(1)} %add.27.a0_hbm), channel_id=1, source_target_pairs={{0,16},{1,17},{2,18},{3,19},{4,20},{5,21},{6,22},{7,23},{8,24},{9,... | collective-permute-start | bytes 393224 | tf_op jit(solution)/shard_map/ppermute | solution.py:223
  49.0 9.3 %collective-permute-start.7 = (bf16[2,32,1024]{2,1,0:T(8,128)(2,1)S(1)}, bf16[2,32,1024]{2,1,0:T(8,128)(2,1)S(1)}, u32[]{:S(2)}, u32[]{:S(2)}) collective-permute-start(bf16[2,32,1024]{2,1,0:T(8,128)(2,1)S(1)} %add.27.a0_hbm), channel_id=1, source_target_pairs={{0,8},{1,9},{2,10},{3,11},{4,12},{5,13},{6,14},{7,15},{8,16},{9,17... | collective-permute-start | bytes 393224 | tf_op jit(solution)/shard_map/ppermute | solution.py:223
  50.0 20.1 %all-to-all-start.1 = ((f16[32,40,128]{2,1,0:T(8,128)(2,1)}), f16[32,40,128]{2,1,0:T(8,128)(2,1)S(1)}, u32[]{:S(2)}, u32[]{:S(2)}) async-start(f16[32,40,128]{2,1,0:T(8,128)(2,1)} %convert_element_type.8), calls=%async_computation.1 | async-start | bytes 655360 | tf_op jit(solution)/shard_map/all_to_all | solution.py:259
  58.2 0.6 copy-start.2
  58.2 0.7 copy-start.3
  58.9 0.6 copy-start.4

commit v3 on v2

--- a/solution.py
+++ b/solution.py
@@ -205,16 +205,19 @@
     return mine
 
 
+FAN = (2, 6, 5)
+
+
 def fan_along_z(mine):
     root = mine
-    for step in (4, 2, 6):
+    for step in FAN:
         mine = mine + lax.ppermute(root, "ctx", [(at(y, 0), at(y, step)) for y in range(QUARTERS)])
     return mine
 
 
 def pair_along_z(mine):
-    pairs = [(at(y, z), at(y, z + 1)) for y in range(QUARTERS) for z in range(0, KV_HEADS, 2)]
-    return mine + lax.ppermute(mine, "ctx", pairs)
+    pairs = [(at(y, z), at(y, z ^ 1)) for y in range(QUARTERS) for z in (0,) + FAN]
+    return lax.ppermute(mine, "ctx", pairs)
 
 
 def gather_along_y(mine):
@@ -244,8 +247,9 @@
     quarter = scatter_anchor(context_key_value)
     received = lax.all_to_all(packed, "ctx", 0, 0)
     quarter = fan_along_z(quarter)
+    from_pair = pair_along_z(quarter)
     received, quarter = lax.optimization_barrier((received, quarter))
-    quarter = pair_along_z(quarter)
+    quarter = quarter + from_pair
     partial = pl.pallas_call(
         query_kernel,
         out_shape=jax.ShapeDtypeStruct((CTX, B_ROWS, D), F32),
@@ -260,7 +264,7 @@
     context_out = pl.pallas_call(
         encode_kernel,
         out_shape=jax.ShapeDtypeStruct(context_q.shape, BF16),
-        in_specs=[SMEM, HBM, HBM] + [ANY] * QUARTERS,
+        in_specs=[SMEM, HBM, HBM] + [VMEM] * QUARTERS,
         out_specs=HBM,
         scratch_shapes=[
             pltpu.VMEM(context_q.shape, BF16),
@@ -270,7 +274,7 @@
             pltpu.SemaphoreType.DMA((QUARTERS + 1,)),
             pltpu.SemaphoreType.DMA((KV_HEADS,)),
         ],
-        compiler_params=pltpu.CompilerParams(vmem_limit_bytes=56 * 1024 * 1024),
+        compiler_params=pltpu.CompilerParams(vmem_limit_bytes=52 * 1024 * 1024),
         cost_estimate=cost(1 << 36, 1 << 24),
     )(place, context_q, context_key_value, *anchor)
     query_out = pl.pallas_call(

time: 71.5 us -> 69.7 us (0.975)
  starting transfers between devices: 27.9 us -> 29.8 us
  waiting for transfers between devices: 26.7 us -> 24.9 us
  local copies, waits for them, and re-layouts: 1.34 us -> 0.03 us
    all_to_all x1, waiting for transfers between devices: 20.8 us -> 19 us  [per_device(): received = lax.all_to_all(packed, 'ctx', 0, 0)]
    ppermute x1, waiting for transfers between devices: 3.12 us -> 1.33 us  [pair_along_z(): return lax.ppermute(mine, 'ctx', pairs)]
    all_to_all x1, waiting for transfers between devices: 2.77 us -> 4.56 us  [per_device(): lax.all_to_all(partial.astype(jnp.float16), 'ctx', 0, 0).astype(F32)]
    ppermute x3, starting transfers between devices: 3.01 us -> 4.65 us  [gather_along_y(): lax.ppermute(mine, 'ctx', [(at(y, z), at((y + k) % QUARTERS, z)) for y, z...]
    unnamed x10 -> x2, local copies, waits for them, and re-layouts: 1.31 us -> 0.01 us
where the time goes in v3:
time: 69.7 us; the launch traced here: 69.3 us
  starting transfers between devices  29.8 us (43%)
  waiting for transfers between devices  24.9 us (36%)
  Pallas kernels  12.8 us (18%)
  other arithmetic  0.9 us (1%)
  between operations  0.85 us (1%)
    all_to_all x1, waiting for transfers between devices, per_device(): received = lax.all_to_all(packed, 'ctx', 0, 0)  19 us
    all_to_all x1, starting transfers between devices, per_device(): received = lax.all_to_all(packed, 'ctx', 0, 0)  11.4 us
    all_to_all x1, starting transfers between devices, per_device(): lax.all_to_all(partial.astype(jnp.float16), 'ctx', 0, 0).astype(F32)  8.44 us
    pallas_call x1, Pallas kernels, per_device(): pl.pallas_call(encode_kernel, out_shape=jax.ShapeDtypeStruct(context_q.sh...  7.33 us
    ppermute x3, starting transfers between devices, gather_along_y(): lax.ppermute(mine, 'ctx', [(at(y, z), at((y + k) % QUARTERS, z)) for y, z...  4.65 us
    all_to_all x1, waiting for transfers between devices, per_device(): lax.all_to_all(partial.astype(jnp.float16), 'ctx', 0, 0).astype(F32)  4.56 us
    pallas_call x1, Pallas kernels, per_device(): pl.pallas_call(query_kernel, out_shape=jax.ShapeDtypeStruct((CTX, B_ROWS,...  2.43 us
    pallas_call x1, Pallas kernels, per_device(): pl.pallas_call(pack_kernel, out_shape=jax.ShapeDtypeStruct((CTX, A_ROWS,...  2.21 us
  transfers between devices with their start and end apart: 12, of which 3 were waited for; matrix products, arithmetic and copies ran while one was open for 1% of the time, Pallas kernels for 14%

profile of v3, /device:TPU:36, one launch (start us, length us, event | category | flops | bytes accessed | tf_op | source)
XLA Modules:
  0.0 69.3 jit_solution(11485415915840310033)
XLA Ops:
  0.6 0.0 copy-start
  0.6 2.2 %shard_map.59 = bf16[32,104,128]{2,1,0:T(8,128)(2,1)} custom-call(bf16[2,128,1024]{2,1,0:T(8,128)(2,1)} %kv_hbm.3, bf16[4,8192]{1,0:T(4,128)(2,1)} %q_hbm.2, bf16[2,4,1024]{2,1,0:T(4,128)(2,1)} %qkv_hbm.1), custom_call_target="tpu_custom_call" | custom-call | bytes 2097152 | tf_op jit(solution)/shard_map/pallas_call | solution.py:233
  2.9 11.4 %all-to-all-start = ((bf16[32,104,128]{2,1,0:T(8,128)(2,1)}), bf16[32,104,128]{2,1,0:T(8,128)(2,1)S(1)}, u32[]{:S(2)}, u32[]{:S(2)}) async-start(bf16[32,104,128]{2,1,0:T(8,128)(2,1)} %shard_map.59), calls=%async_computation | async-start | bytes 1703936 | tf_op jit(solution)/shard_map/all_to_all | solution.py:248
  14.2 0.0 copy-done
  14.3 0.7 collective-permute-start
  15.0 0.7 collective-permute-start.1
  15.6 0.7 collective-permute-start.2
  16.3 0.0 collective-permute-done
  16.3 0.0 collective-permute-done.1
  16.3 0.0 collective-permute-done.2
  16.4 0.7 collective-permute-start.5
  17.1 0.7 collective-permute-start.4
  17.7 0.7 collective-permute-start.3
  18.4 0.0 collective-permute-done.5
  18.4 0.0 collective-permute-done.4
  18.4 0.0 collective-permute-done.3
  18.5 1.3 %collective-permute-start.6 = (bf16[2,32,1024]{2,1,0:T(8,128)(2,1)S(1)}, bf16[2,32,1024]{2,1,0:T(8,128)(2,1)S(1)}, u32[]{:S(2)}, u32[]{:S(2)}) collective-permute-start(bf16[2,32,1024]{2,1,0:T(8,128)(2,1)S(1)} %add_add_fusion), channel_id=1, source_target_pairs={{0,1},{2,3},{6,7},{5,4},{8,9},{10,11},{14,15},{13,12},{16,17},{18,... | collective-permute-start | bytes 393224 | tf_op jit(solution)/shard_map/ppermute | solution.py:220
  19.8 19.0 %all-to-all-done.in_ref = bf16[32,104,128]{2,1,0:T(8,128)(2,1)S(1)} async-done(((bf16[32,104,128]{2,1,0:T(8,128)(2,1)}), bf16[32,104,128]{2,1,0:T(8,128)(2,1)S(1)}, u32[]{:S(2)}, u32[]{:S(2)}) %all-to-all-start) | async-done | bytes 852000 | tf_op jit(solution)/shard_map/all_to_all | solution.py:248
  38.8 2.4 %shard_map.60 = f32[32,40,128]{2,1,0:T(8,128)S(1)} custom-call(s32[1]{0:T(128)} %bitcast.place_ref, bf16[32,104,128]{2,1,0:T(8,128)(2,1)S(1)} %all-to-all-done.in_ref), custom_call_target="tpu_custom_call" | custom-call | flops 536870912 | bytes 2097152 | tf_op jit(solution)/shard_map/pallas_call | solution.py:253
  41.2 1.3 %collective-permute-done.6 = bf16[2,32,1024]{2,1,0:T(8,128)(2,1)S(1)} collective-permute-done((bf16[2,32,1024]{2,1,0:T(8,128)(2,1)S(1)}, bf16[2,32,1024]{2,1,0:T(8,128)(2,1)S(1)}, u32[]{:S(2)}, u32[]{:S(2)}) %collective-permute-start.6) | collective-permute-done | bytes 131104 | tf_op jit(solution)/shard_map/ppermute | solution.py:220
  42.6 3.0 %collective-permute-start.9 = (bf16[2,32,1024]{2,1,0:T(8,128)(2,1)S(1)}, bf16[2,32,1024]{2,1,0:T(8,128)(2,1)S(1)}, u32[]{:S(2)}, u32[]{:S(2)}) collective-permute-start(bf16[2,32,1024]{2,1,0:T(8,128)(2,1)S(1)} %add.27.a0_hbm), channel_id=1, source_target_pairs={{0,24},{1,25},{2,26},{3,27},{4,28},{5,29},{6,30},{7,31},{8,0},{9,1... | collective-permute-start | bytes 393224 | tf_op jit(solution)/shard_map/ppermute | solution.py:226
  45.5 0.8 %collective-permute-start.8 = (bf16[2,32,1024]{2,1,0:T(8,128)(2,1)S(1)}, bf16[2,32,1024]{2,1,0:T(8,128)(2,1)S(1)}, u32[]{:S(2)}, u32[]{:S(2)}) collective-permute-start(bf16[2,32,1024]{2,1,0:T(8,128)(2,1)S(1)} %add.27.a0_hbm), channel_id=1, source_target_pairs={{0,16},{1,17},{2,18},{3,19},{4,20},{5,21},{6,22},{7,23},{8,24},{9,... | collective-permute-start | bytes 393224 | tf_op jit(solution)/shard_map/ppermute | solution.py:226
  46.3 0.9 %collective-permute-start.7 = (bf16[2,32,1024]{2,1,0:T(8,128)(2,1)S(1)}, bf16[2,32,1024]{2,1,0:T(8,128)(2,1)S(1)}, u32[]{:S(2)}, u32[]{:S(2)}) collective-permute-start(bf16[2,32,1024]{2,1,0:T(8,128)(2,1)S(1)} %add.27.a0_hbm), channel_id=1, source_target_pairs={{0,8},{1,9},{2,10},{3,11},{4,12},{5,13},{6,14},{7,15},{8,16},{9,17... | collective-permute-start | bytes 393224 | tf_op jit(solution)/shard_map/ppermute | solution.py:226
  47.2 0.8 %convert_element_type.8 = f16[32,40,128]{2,1,0:T(8,128)(2,1)} convert(f32[32,40,128]{2,1,0:T(8,128)S(1)} %shard_map.60) | non-fusion elementwise | flops 163840 | bytes 983040 | tf_op jit(solution)/shard_map/convert_element_type | solution.py:263
  48.0 8.4 %all-to-all-start.1 = ((f16[32,40,128]{2,1,0:T(8,128)(2,1)}), f16[32,40,128]{2,1,0:T(8,128)(2,1)S(1)}, u32[]{:S(2)}, u32[]{:S(2)}) async-start(f16[32,40,128]{2,1,0:T(8,128)(2,1)} %convert_element_type.8), calls=%async_computation.1 | async-start | bytes 655360 | tf_op jit(solution)/shard_map/all_to_all | solution.py:263
  56.4 0.0 collective-permute-done.9.a3_hbm
  56.4 0.0 collective-permute-done.8.a2_hbm
  56.4 0.0 collective-permute-done.7.a1_hbm
  56.5 7.3 %shard_map.61 = bf16[128,8192]{1,0:T(8,128)(2,1)} custom-call(s32[1]{0:T(128)} %bitcast.place_ref, bf16[128,8192]{1,0:T(8,128)(2,1)} %q_hbm.3, bf16[2,128,1024]{2,1,0:T(8,128)(2,1)S(1)} %copy-done, bf16[2,32,1024]{2,1,0:T(8,128)(2,1)S(1)} %add.27.a0_hbm, bf16[2,32,1024]{2,1,0:T(8,128)(2,1)S(1)} %collective-permute-done.7.a1_hbm, ...), custom_call_target="tpu_custom_call" | custom-call | flops 68719476736 | bytes 16777216 | tf_op jit(solution)/shard_map/pallas_call | solution.py:264
  63.8 4.6 %all-to-all-done.1 = f16[32,40,128]{2,1,0:T(8,128)(2,1)S(1)} async-done(((f16[32,40,128]{2,1,0:T(8,128)(2,1)}), f16[32,40,128]{2,1,0:T(8,128)(2,1)S(1)}, u32[]{:S(2)}, u32[]{:S(2)}) %all-to-all-start.1) | async-done | bytes 327712 | tf_op jit(solution)/shard_map/all_to_all | solution.py:263
  68.4 0.9 %shard_map.62 = bf16[4,8192]{1,0:T(4,128)(2,1)} custom-call(f32[32,40,128]{2,1,0:T(8,128)S(1)} %convert_element_type.9.in_ref), custom_call_target="tpu_custom_call" | custom-call | flops 1048576 | bytes 1048576 | tf_op jit(solution)/shard_map/pallas_call | solution.py:280
  (5 shorter events, 0.2 us)
Async XLA Ops:
  0.6 13.6 %copy-start = (bf16[2,128,1024]{2,1,0:T(8,128)(2,1)S(1)}, bf16[2,128,1024]{2,1,0:T(8,128)(2,1)}, u32[]{:S(2)}) copy-start(bf16[2,128,1024]{2,1,0:T(8,128)(2,1)} %kv_hbm.3) | copy-start | bytes 1572868
  2.9 35.9 %all-to-all-start = ((bf16[32,104,128]{2,1,0:T(8,128)(2,1)}), bf16[32,104,128]{2,1,0:T(8,128)(2,1)S(1)}, u32[]{:S(2)}, u32[]{:S(2)}) async-start(bf16[32,104,128]{2,1,0:T(8,128)(2,1)} %shard_map.59), calls=%async_computation | async-start | bytes 1703936 | tf_op jit(solution)/shard_map/all_to_all | solution.py:248
  14.3 2.0 %collective-permute-start = (bf16[2,32,1024]{2,1,0:T(8,128)(2,1)S(1)}, bf16[2,32,1024]{2,1,0:T(8,128)(2,1)S(1)}, u32[]{:S(2)}, u32[]{:S(2)}) collective-permute-start(bf16[2,32,1024]{2,1,0:T(8,128)(2,1)S(1)} %get-tuple-element.10), channel_id=1, source_target_pairs={{0,8},{32,40},{64,72},{96,104},{128,136},{160,168},{192,200},{224,... | collective-permute-start | bytes 393224 | tf_op jit(solution)/shard_map/ppermute | solution.py:204
  15.0 1.4 %collective-permute-start.1 = (bf16[2,32,1024]{2,1,0:T(8,128)(2,1)S(1)}, bf16[2,32,1024]{2,1,0:T(8,128)(2,1)S(1)}, u32[]{:S(2)}, u32[]{:S(2)}) collective-permute-start(bf16[2,32,1024]{2,1,0:T(8,128)(2,1)S(1)} %get-tuple-element.11), channel_id=1, source_target_pairs={{0,16},{32,48},{64,80},{96,112},{128,144},{160,176},{192,208},{224... | collective-permute-start | bytes 393224 | tf_op jit(solution)/shard_map/ppermute | solution.py:204
  15.6 0.7 %collective-permute-start.2 = (bf16[2,32,1024]{2,1,0:T(8,128)(2,1)S(1)}, bf16[2,32,1024]{2,1,0:T(8,128)(2,1)S(1)}, u32[]{:S(2)}, u32[]{:S(2)}) collective-permute-start(bf16[2,32,1024]{2,1,0:T(8,128)(2,1)S(1)} %get-tuple-element.12), channel_id=1, source_target_pairs={{0,24},{32,56},{64,88},{96,120},{128,152},{160,184},{192,216},{224... | collective-permute-start | bytes 393224 | tf_op jit(solution)/shard_map/ppermute | solution.py:204
  16.4 2.0 %collective-permute-start.5 = (bf16[2,32,1024]{2,1,0:T(8,128)(2,1)S(1)}, bf16[2,32,1024]{2,1,0:T(8,128)(2,1)S(1)}, u32[]{:S(2)}, u32[]{:S(2)}) collective-permute-start(bf16[2,32,1024]{2,1,0:T(8,128)(2,1)S(1)} %add_add_fusion.1), channel_id=1, source_target_pairs={{0,5},{8,13},{16,21},{24,29},{32,37},{40,45},{48,53},{56,61},{64,6... | collective-permute-start | bytes 393224 | tf_op jit(solution)/shard_map/ppermute | solution.py:214
  17.1 1.4 %collective-permute-start.4 = (bf16[2,32,1024]{2,1,0:T(8,128)(2,1)S(1)}, bf16[2,32,1024]{2,1,0:T(8,128)(2,1)S(1)}, u32[]{:S(2)}, u32[]{:S(2)}) collective-permute-start(bf16[2,32,1024]{2,1,0:T(8,128)(2,1)S(1)} %add_add_fusion.1), channel_id=1, source_target_pairs={{0,6},{8,14},{16,22},{24,30},{32,38},{40,46},{48,54},{56,62},{64,7... | collective-permute-start | bytes 393224 | tf_op jit(solution)/shard_map/ppermute | solution.py:214
  17.7 0.7 %collective-permute-start.3 = (bf16[2,32,1024]{2,1,0:T(8,128)(2,1)S(1)}, bf16[2,32,1024]{2,1,0:T(8,128)(2,1)S(1)}, u32[]{:S(2)}, u32[]{:S(2)}) collective-permute-start(bf16[2,32,1024]{2,1,0:T(8,128)(2,1)S(1)} %add_add_fusion.1), channel_id=1, source_target_pairs={{0,2},{8,10},{16,18},{24,26},{32,34},{40,42},{48,50},{56,58},{64,6... | collective-permute-start | bytes 393224 | tf_op jit(solution)/shard_map/ppermute | solution.py:214
  18.5 24.0 %collective-permute-start.6 = (bf16[2,32,1024]{2,1,0:T(8,128)(2,1)S(1)}, bf16[2,32,1024]{2,1,0:T(8,128)(2,1)S(1)}, u32[]{:S(2)}, u32[]{:S(2)}) collective-permute-start(bf16[2,32,1024]{2,1,0:T(8,128)(2,1)S(1)} %add_add_fusion), channel_id=1, source_target_pairs={{0,1},{2,3},{6,7},{5,4},{8,9},{10,11},{14,15},{13,12},{16,17},{18,... | collective-permute-start | bytes 393224 | tf_op jit(solution)/shard_map/ppermute | solution.py:220
  42.6 13.9 %collective-permute-start.9 = (bf16[2,32,1024]{2,1,0:T(8,128)(2,1)S(1)}, bf16[2,32,1024]{2,1,0:T(8,128)(2,1)S(1)}, u32[]{:S(2)}, u32[]{:S(2)}) collective-permute-start(bf16[2,32,1024]{2,1,0:T(8,128)(2,1)S(1)} %add.27.a0_hbm), channel_id=1, source_target_pairs={{0,24},{1,25},{2,26},{3,27},{4,28},{5,29},{6,30},{7,31},{8,0},{9,1... | collective-permute-start | bytes 393224 | tf_op jit(solution)/shard_map/ppermute | solution.py:226
  45.5 10.9 %collective-permute-start.8 = (bf16[2,32,1024]{2,1,0:T(8,128)(2,1)S(1)}, bf16[2,32,1024]{2,1,0:T(8,128)(2,1)S(1)}, u32[]{:S(2)}, u32[]{:S(2)}) collective-permute-start(bf16[2,32,1024]{2,1,0:T(8,128)(2,1)S(1)} %add.27.a0_hbm), channel_id=1, source_target_pairs={{0,16},{1,17},{2,18},{3,19},{4,20},{5,21},{6,22},{7,23},{8,24},{9,... | collective-permute-start | bytes 393224 | tf_op jit(solution)/shard_map/ppermute | solution.py:226
  46.3 10.1 %collective-permute-start.7 = (bf16[2,32,1024]{2,1,0:T(8,128)(2,1)S(1)}, bf16[2,32,1024]{2,1,0:T(8,128)(2,1)S(1)}, u32[]{:S(2)}, u32[]{:S(2)}) collective-permute-start(bf16[2,32,1024]{2,1,0:T(8,128)(2,1)S(1)} %add.27.a0_hbm), channel_id=1, source_target_pairs={{0,8},{1,9},{2,10},{3,11},{4,12},{5,13},{6,14},{7,15},{8,16},{9,17... | collective-permute-start | bytes 393224 | tf_op jit(solution)/shard_map/ppermute | solution.py:226
  48.0 20.4 %all-to-all-start.1 = ((f16[32,40,128]{2,1,0:T(8,128)(2,1)}), f16[32,40,128]{2,1,0:T(8,128)(2,1)S(1)}, u32[]{:S(2)}, u32[]{:S(2)}) async-start(f16[32,40,128]{2,1,0:T(8,128)(2,1)} %convert_element_type.8), calls=%async_computation.1 | async-start | bytes 655360 | tf_op jit(solution)/shard_map/all_to_all | solution.py:263

commit v4 on v3

v4 whole, which is shorter than its diff:
```python
import functools

import jax
import jax.numpy as jnp
from jax import lax
from jax.experimental import pallas as pl
from jax.experimental.pallas import tpu as pltpu
from jax.sharding import PartitionSpec as P

KV_HEADS = 8
GROUP = 8
D = 128
BLOCK = 128
YS = 4
PAIRS = 4
SIDES = 2
CTX = YS * PAIRS * SIDES
ROWS = 4
QROWS = ROWS * GROUP
F32 = jnp.float32
BF16 = jnp.bfloat16
FILLER = -1e30
LOG2E = 1.4426950408889634
SCALE = D ** -0.5 * LOG2E

STEPS = [(dy, flip) for dy in range(YS) for flip in range(SIDES)]
A_K, A_V, A_SK, A_SV = 0, BLOCK, 2 * BLOCK, 2 * BLOCK + 8
A_ROWS = A_SV + 8
B_S = QROWS
B_ROWS = B_S + 8


def dot_nt(a, b):
    return lax.dot_general(a, b, (((1,), (1,)), ((), ())), preferred_element_type=F32)


def dot_nn(a, b):
    return lax.dot_general(a, b, (((1,), (0,)), ((), ())), preferred_element_type=F32)


def pack_kernel(place_ref, kv_hbm, q_hbm, qkv_hbm, *refs):
    kv_out_refs, (q_out_ref, kv_ref, q_ref, qkv_ref, sems) = refs[:KV_HEADS], refs[KV_HEADS:]
    copies = [
        pltpu.make_async_copy(source, target, sems.at[i])
        for i, (source, target) in enumerate(((q_hbm, q_ref), (qkv_hbm, qkv_ref), (kv_hbm, kv_ref)))
    ]
    for copy in copies:
        copy.start()
    for copy in copies:
        copy.wait()
    q = q_ref[...].astype(F32)
    for head in range(KV_HEADS):
        first = head * GROUP * D
        queries = jnp.concatenate(
            [q[:, first + j * D:first + (j + 1) * D] for j in range(GROUP)], 0
        ).astype(BF16)
        for pair in range(PAIRS):
            q_out_ref[head // SIDES * PAIRS * SIDES + pair * SIDES + head % SIDES] = queries
    y, side = place_ref[0] // (PAIRS * SIDES), place_ref[0] % SIDES
    blank = jnp.zeros((8 - ROWS, D), F32)
    for (dy, flip), out_ref in zip(STEPS, kv_out_refs):
        head = (y + dy) % YS * SIDES + (side + flip) % SIDES
        lanes = pl.ds(pl.multiple_of(head * D, D), D)
        out_ref[A_K:A_K + BLOCK, :] = kv_ref[0, :, lanes]
        out_ref[A_V:A_V + BLOCK, :] = kv_ref[1, :, lanes]
        out_ref[A_SK:A_ROWS, :] = jnp.concatenate(
            [qkv_ref[0, :, lanes].astype(F32), blank, qkv_ref[1, :, lanes].astype(F32), blank], 0
        ).astype(BF16)


CHUNK = 8
STACK = 4


def query_kernel(place_ref, *refs):
    kv_refs, (q_ref, out_ref) = refs[:KV_HEADS], refs[KV_HEADS:]
    place = place_ref[0]
    y, pair, side = place // (PAIRS * SIDES), place // SIDES % PAIRS, place % SIDES
    keys = jnp.concatenate([ref[A_K:A_K + BLOCK, :] for ref in kv_refs], 0)
    values = jnp.concatenate([ref[A_V:A_V + BLOCK, :] for ref in kv_refs], 0)
    tails = [ref[A_SK:A_ROWS, :].astype(F32) for ref in kv_refs]
    self_keys = jnp.concatenate([tail[0:8] for tail in tails], 0).astype(BF16)
    self_values = jnp.concatenate([tail[8:16] for tail in tails], 0).astype(BF16)
    rows = CHUNK * QROWS
    row_id = lax.broadcasted_iota(jnp.int32, (rows, KV_HEADS * 8), 0)
    column = lax.broadcasted_iota(jnp.int32, (rows, KV_HEADS * 8), 1)
    source, key_row = column // 8, column % 8
    source_y, source_side = (y + YS - source // SIDES) % YS, (side + source % SIDES) % SIDES
    key_pos = (source_y * (PAIRS * SIDES) + pair * SIDES + source_side) * ROWS + key_row
    key_pos = jnp.where(key_row < ROWS, key_pos, CTX * ROWS)
    row_pos = (row_id // QROWS) * ROWS + row_id % ROWS
    diagonal = (
        lax.broadcasted_iota(jnp.int32, (CHUNK, QROWS, D), 1)
        == lax.broadcasted_iota(jnp.int32, (CHUNK, QROWS, D), 2)
    )
    for chunk in range(CTX // CHUNK):
        sources = slice(chunk * CHUNK, (chunk + 1) * CHUNK)
        queries = q_ref[sources].reshape(rows, D)
        scores = dot_nt(queries, keys)
        self_scores = dot_nt(queries, self_keys)
        self_scores = jnp.where(key_pos <= row_pos + chunk * CHUNK * ROWS, self_scores, FILLER)
        highest = jnp.maximum(jnp.max(scores, 1, keepdims=True), jnp.max(self_scores, 1, keepdims=True))
        weights = jnp.exp2((scores - highest) * SCALE)
        self_weights = jnp.exp2((self_scores - highest) * SCALE)
        total = jnp.sum(weights, 1, keepdims=True) + jnp.sum(self_weights, 1, keepdims=True)
        summed = dot_nn(weights.astype(BF16), values) + dot_nn(self_weights.astype(BF16), self_values)
        out_ref[sources, 0:QROWS, :] = (summed / total).reshape(CHUNK, QROWS, D)
        log_sum = (highest * SCALE + jnp.log2(total)).reshape(CHUNK, QROWS, 1)
        log_row = jnp.sum(jnp.where(diagonal, log_sum, 0.0), 1, keepdims=True)
        first = log_row.astype(BF16).astype(F32)
        second = (log_row - first).astype(BF16).astype(F32)
        third = log_row - first - second
        out_ref[sources, B_S:B_ROWS, :] = jnp.concatenate(
            [first, second, third, jnp.zeros((CHUNK, 5, D), F32)], 1
        )


def encode_kernel(
    place_ref, q_hbm, kv_hbm, a0_ref, a1_ref, a2_ref, a3_ref, out_hbm,
    q_ref, kv_ref, anchor_ref, out_ref, q_sems, kv_sems, sems
):
    width = GROUP * D
    y = place_ref[0] // (PAIRS * SIDES)

    def copy_in(head):
        lanes = pl.ds(pl.multiple_of(head * width, width), width)
        return pltpu.make_async_copy(q_hbm.at[:, lanes], q_ref.at[:, lanes], q_sems.at[head])

    def copy_out(head):
        lanes = pl.ds(pl.multiple_of(head * width, width), width)
        return pltpu.make_async_copy(out_ref.at[:, lanes], out_hbm.at[:, lanes], sems.at[head])

    copies = [pltpu.make_async_copy(kv_hbm, kv_ref, kv_sems.at[YS])]
    for dy, source in enumerate((a0_ref, a1_ref, a2_ref, a3_ref)):
        first = (y + YS - dy) % YS * SIDES
        copies.append(pltpu.make_async_copy(source, anchor_ref.at[pl.ds(first, SIDES)], kv_sems.at[dy]))
    for copy in copies:
        copy.start()
    for head in range(KV_HEADS):
        copy_in(head).start()
    filler = jnp.where(place_ref[0] > 0, 0, BLOCK)
    row = lax.broadcasted_iota(jnp.int32, (BLOCK, 2 * BLOCK), 0)
    column = lax.broadcasted_iota(jnp.int32, (BLOCK, 2 * BLOCK), 1)
    allowed = (column >= filler) & (column <= row + BLOCK)
    for copy in copies:
        copy.wait()

    def one_head(head, carry):
        copy_in(head).wait()
        kv_lanes = pl.ds(pl.multiple_of(head * D, D), D)
        keys = jnp.concatenate([anchor_ref[head, A_K:A_K + BLOCK, :], kv_ref[0, :, kv_lanes]], 0)
        values = jnp.concatenate([anchor_ref[head, A_V:A_V + BLOCK, :], kv_ref[1, :, kv_lanes]], 0)
        for first in range(0, GROUP, STACK):
            lanes = [pl.ds(pl.multiple_of(head * width + (first + j) * D, D), D) for j in range(STACK)]
            queries = jnp.concatenate([q_ref[:, each] for each in lanes], 0)
            scores = dot_nt(queries, keys).reshape(STACK, BLOCK, 2 * BLOCK)
            scores = jnp.where(allowed[None], scores, FILLER)
            highest = jnp.max(scores, 2, keepdims=True)
            weights = jnp.exp2((scores - highest) * SCALE)
            total = jnp.sum(weights, 2, keepdims=True)
            summed = dot_nn(weights.astype(BF16).reshape(STACK * BLOCK, 2 * BLOCK), values)
            attended = (summed.reshape(STACK, BLOCK, D) / total).astype(BF16)
            for j in range(STACK):
                out_ref[:, lanes[j]] = attended[j]
        copy_out(head).start()
        return carry

    lax.fori_loop(0, KV_HEADS, one_head, 0)
    for head in range(KV_HEADS):
        copy_out(head).wait()


def merge_kernel(in_ref, out_ref):
    diagonal = (
        lax.broadcasted_iota(jnp.int32, (KV_HEADS, QROWS, D), 1)
        == lax.broadcasted_iota(jnp.int32, (KV_HEADS, QROWS, D), 2)
    )
    received = in_ref[...].reshape(YS, PAIRS, SIDES, B_ROWS, D)
    logs = []
    for pair in range(PAIRS):
        parts = received[:, pair, :, B_S:, :].reshape(KV_HEADS, B_ROWS - B_S, D)
        logs.append(parts[:, 0:1, :] + parts[:, 1:2, :] + parts[:, 2:3, :])
    highest = functools.reduce(jnp.maximum, logs)
    shares = [jnp.exp2(log - highest) for log in logs]
    whole = functools.reduce(jnp.add, shares)
    merged = jnp.zeros((KV_HEADS, QROWS, D), F32)
    for pair in range(PAIRS):
        share = jnp.sum(jnp.where(diagonal, shares[pair] / whole, 0.0), 2, keepdims=True)
        merged = merged + share * received[:, pair, :, 0:QROWS, :].reshape(KV_HEADS, QROWS, D)
    for head in range(KV_HEADS):
        for j in range(GROUP):
            first = (head * GROUP + j) * D
            out_ref[:, first:first + D] = merged[head, j * ROWS:(j + 1) * ROWS, :].astype(BF16)


VMEM = pl.BlockSpec(memory_space=pltpu.VMEM)
ANY = pl.BlockSpec(memory_space=pl.ANY)
SMEM = pl.BlockSpec(memory_space=pltpu.SMEM)
HBM = pl.BlockSpec(memory_space=pltpu.HBM)
PARAMS = pltpu.CompilerParams(vmem_limit_bytes=32 * 1024 * 1024)


def cost(flops, nbytes):
    return pl.CostEstimate(flops=flops, bytes_accessed=nbytes, transcendentals=0)


def at(y, z):
    return y * PAIRS * SIDES + z


ALL = [(y, z) for y in range(YS) for z in range(PAIRS * SIDES)]


def fan_along_z(piece):
    result = piece
    for step in (2, 6, 4):
        pairs = [(at(y, side), at(y, side + step)) for y in range(YS) for side in range(SIDES)]
        result = result + lax.ppermute(piece, "ctx", pairs)
    return result


def step_in_pair(array, dy, flip):
    return lax.ppermute(array, "ctx", [(at(y, z), at((y + dy) % YS, z ^ flip)) for y, z in ALL])


def per_device(context_q, context_key_value, query_token_queries, query_key_value):
    index = lax.axis_index("ctx")
    place = index.astype(jnp.int32).reshape(1)
    y, side = index // (PAIRS * SIDES), index % SIDES
    *packed_kv, packed_q = pl.pallas_call(
        pack_kernel,
        out_shape=(jax.ShapeDtypeStruct((A_ROWS, D), BF16),) * KV_HEADS
        + (jax.ShapeDtypeStruct((CTX, QROWS, D), BF16),),
        in_specs=[SMEM, HBM, HBM, HBM],
        out_specs=(VMEM,) * (KV_HEADS + 1),
        scratch_shapes=[
            pltpu.VMEM(context_key_value.shape, BF16),
            pltpu.VMEM(query_token_queries.shape, BF16),
            pltpu.VMEM(query_key_value.shape, BF16),
            pltpu.SemaphoreType.DMA((3,)),
        ],
        compiler_params=pltpu.CompilerParams(vmem_limit_bytes=56 * 1024 * 1024),
        cost_estimate=cost(0, 1 << 21),
    )(place, context_key_value, query_token_queries, query_key_value)
    queries = lax.all_to_all(packed_q, "ctx", 0, 0)
    kv = [packed_kv[0]] + [step_in_pair(packed_kv[n], *STEPS[n]) for n in range(1, KV_HEADS)]
    in_first = index // SIDES % PAIRS == 0
    piece = sum(
        jnp.where(in_first & (y == dy) & (side == flip), kv[n][:2 * BLOCK], 0)
        for n, (dy, flip) in enumerate(STEPS)
    )
    piece = fan_along_z(piece)
    other = step_in_pair(piece, 0, 1)
    partial = pl.pallas_call(
        query_kernel,
        out_shape=jax.ShapeDtypeStruct((CTX, B_ROWS, D), F32),
        in_specs=[SMEM] + [VMEM] * (KV_HEADS + 1),
        out_specs=VMEM,
        compiler_params=PARAMS,
        cost_estimate=cost(1 << 29, 1 << 21),
    )(place, *kv, queries)
    halved = partial.astype(jnp.float16)
    halved, piece = lax.optimization_barrier((halved, piece))
    both = jnp.stack([jnp.where(side == 0, piece, other), jnp.where(side == 0, other, piece)])
    pieces = [both] + [step_in_pair(both, dy, 0) for dy in range(1, YS)]
    gathered = lax.all_to_all(halved, "ctx", 0, 0).astype(F32)
    context_out = pl.pallas_call(
        encode_kernel,
        out_shape=jax.ShapeDtypeStruct(context_q.shape, BF16),
        in_specs=[SMEM, HBM, HBM] + [VMEM] * YS,
        out_specs=HBM,
        scratch_shapes=[
            pltpu.VMEM(context_q.shape, BF16),
            pltpu.VMEM(context_key_value.shape, BF16),
            pltpu.VMEM((KV_HEADS, 2 * BLOCK, D), BF16),
            pltpu.VMEM(context_q.shape, BF16),
            pltpu.SemaphoreType.DMA((KV_HEADS,)),
            pltpu.SemaphoreType.DMA((YS + 1,)),
            pltpu.SemaphoreType.DMA((KV_HEADS,)),
        ],
        compiler_params=pltpu.CompilerParams(vmem_limit_bytes=52 * 1024 * 1024),
        cost_estimate=cost(1 << 36, 1 << 24),
    )(place, context_q, context_key_value, *pieces)
    query_out = pl.pallas_call(
        merge_kernel,
        out_shape=jax.ShapeDtypeStruct(query_token_queries.shape, BF16),
        in_specs=[VMEM],
        out_specs=VMEM,
        compiler_params=PARAMS,
        cost_estimate=cost(1 << 20, 1 << 20),
    )(gathered)
    return context_out, query_out


def solution(mesh):
    return jax.shard_map(
        per_device,
        mesh=mesh,
        in_specs=(
            P(("req", "ctx"), None),
            P(None, ("req", "ctx"), None),
            P(("req", "ctx"), None),
            P(None, ("req", "ctx"), None),
        ),
        out_specs=(P(("req", "ctx"), None), P(("req", "ctx"), None)),
        check_vma=False,
    )
```

time: 69.7 us -> 67.5 us (0.968)
  waiting for transfers between devices: 24.9 us -> 5.98 us
  starting transfers between devices: 29.8 us -> 44.3 us
  other arithmetic: 0.9 us -> 1.77 us
  local copies, waits for them, and re-layouts: 0.03 us -> 0.89 us
    all_to_all x2, waiting for transfers between devices: 23.5 us -> 4.07 us  [the longest x1 4.07 us: per_device(): gathered = lax.all_to_all(halved, 'ctx', 0, 0).astype(F32)]
    ppermute x10 -> x14, starting transfers between devices: 9.95 us -> 26.2 us  [the longest x11 17.3 us: step_in_pair(): lax.ppermute(array, 'ctx', [(at(y, z), at((y + dy) % YS, z ^ flip)) for y...]
    all_to_all x2, starting transfers between devices: 19.8 us -> 18.1 us  [the longest x1 10.1 us: per_device(): queries = lax.all_to_all(packed_q, 'ctx', 0, 0)]
    unnamed x2 -> x4, local copies, waits for them, and re-layouts: 0.01 us -> 0.89 us
    add x3 -> x2, other arithmetic: 0.09 us -> 0.92 us  [the longest x1 0.9 us: per_device(): sum((jnp.where(in_first & (y == dy) & (side == flip), kv[n][:2 * BLOCK],...]
    ppermute x10 -> x14, waiting for transfers between devices: 1.36 us -> 1.91 us  [the longest x3 1.88 us: fan_along_z(): result = result + lax.ppermute(piece, 'ctx', pairs)]
  transfers between devices with their start and end apart: 12 -> 16, of which waited for: 3 -> 3; matrix products, arithmetic and copies ran while one was open for 1% -> 3% of each run, Pallas kernels for 14% -> 15%
where the time goes in v4:
time: 67.5 us; the launch traced here: 67 us
  starting transfers between devices  44.3 us (66%)
  Pallas kernels  13.2 us (20%)
  waiting for transfers between devices  5.98 us (9%)
  other arithmetic  1.77 us (3%)
  local copies, waits for them, and re-layouts  0.89 us (1%)
  between operations  0.88 us (1%)
    ppermute x11, starting transfers between devices, step_in_pair(): lax.ppermute(array, 'ctx', [(at(y, z), at((y + dy) % YS, z ^ flip)) for y...  17.3 us
    all_to_all x1, starting transfers between devices, per_device(): queries = lax.all_to_all(packed_q, 'ctx', 0, 0)  10.1 us
    ppermute x3, starting transfers between devices, fan_along_z(): result = result + lax.ppermute(piece, 'ctx', pairs)  8.97 us
    all_to_all x1, starting transfers between devices, per_device(): gathered = lax.all_to_all(halved, 'ctx', 0, 0).astype(F32)  7.95 us
    pallas_call x1, Pallas kernels, per_device(): pl.pallas_call(encode_kernel, out_shape=jax.ShapeDtypeStruct(context_q.sh...  7.68 us
    all_to_all x1, waiting for transfers between devices, per_device(): gathered = lax.all_to_all(halved, 'ctx', 0, 0).astype(F32)  4.07 us
    pallas_call x1, Pallas kernels, per_device(): pl.pallas_call(query_kernel, out_shape=jax.ShapeDtypeStruct((CTX, B_ROWS,...  2.47 us
    pallas_call x1, Pallas kernels, per_device(): pl.pallas_call(pack_kernel, out_shape=(jax.ShapeDtypeStruct((A_ROWS, D),...  2.15 us
  transfers between devices with their start and end apart: 16, of which 3 were waited for; matrix products, arithmetic and copies ran while one was open for 3% of the time, Pallas kernels for 15%

profile of v4, /device:TPU:36, one launch (start us, length us, event | category | flops | bytes accessed | tf_op | source)
XLA Modules:
  0.0 67.0 jit_solution(10265618403299512129)
XLA Ops:
  0.6 2.2 %shard_map.59 = (bf16[272,128]{1,0:T(8,128)(2,1)}, bf16[272,128]{1,0:T(8,128)(2,1)}, bf16[272,128]{1,0:T(8,128)(2,1)}, bf16[272,128]{1,0:T(8,128)(2,1)}, bf16[27...) custom-call(s32[1]{0:T(128)} %bitcast.place_ref, ...), custom_call_target="tpu_custom_call" | custom-call | bytes 2097152 | tf_op jit(solution)/shard_map/pallas_call | solution.py:230
  2.8 0.2 collective-permute-start
  3.0 1.6 %collective-permute-start.1 = (bf16[272,128]{1,0:T(8,128)(2,1)}, bf16[272,128]{1,0:T(8,128)(2,1)S(1)}, u32[]{:S(2)}, u32[]{:S(2)}) collective-permute-start(bf16[272,128]{1,0:T(8,128)(2,1)} %get-tuple-element.15), channel_id=1, source_target_pairs={{0,8},{1,9},{2,10},{3,11},{4,12},{5,13},{6,14},{7,15},{8,16},{9,17... | collective-permute-start | bytes 208904 | tf_op jit(solution)/shard_map/ppermute | solution.py:223
  4.6 2.9 %collective-permute-start.2 = (bf16[272,128]{1,0:T(8,128)(2,1)}, bf16[272,128]{1,0:T(8,128)(2,1)S(1)}, u32[]{:S(2)}, u32[]{:S(2)}) collective-permute-start(bf16[272,128]{1,0:T(8,128)(2,1)} %get-tuple-element.16), channel_id=1, source_target_pairs={{0,9},{1,8},{2,11},{3,10},{4,13},{5,12},{6,15},{7,14},{8,17},{9,16... | collective-permute-start | bytes 208904 | tf_op jit(solution)/shard_map/ppermute | solution.py:223
  7.5 1.5 %collective-permute-start.3 = (bf16[272,128]{1,0:T(8,128)(2,1)}, bf16[272,128]{1,0:T(8,128)(2,1)S(1)}, u32[]{:S(2)}, u32[]{:S(2)}) collective-permute-start(bf16[272,128]{1,0:T(8,128)(2,1)} %get-tuple-element.17), channel_id=1, source_target_pairs={{0,16},{1,17},{2,18},{3,19},{4,20},{5,21},{6,22},{7,23},{8,24},{9,... | collective-permute-start | bytes 208904 | tf_op jit(solution)/shard_map/ppermute | solution.py:223
  9.0 1.5 %collective-permute-start.4 = (bf16[272,128]{1,0:T(8,128)(2,1)}, bf16[272,128]{1,0:T(8,128)(2,1)S(1)}, u32[]{:S(2)}, u32[]{:S(2)}) collective-permute-start(bf16[272,128]{1,0:T(8,128)(2,1)} %get-tuple-element.18), channel_id=1, source_target_pairs={{0,17},{1,16},{2,19},{3,18},{4,21},{5,20},{6,23},{7,22},{8,25},{9,... | collective-permute-start | bytes 208904 | tf_op jit(solution)/shard_map/ppermute | solution.py:223
  10.6 0.0 collective-permute-done.refs_1_
  10.6 1.7 %collective-permute-start.5 = (bf16[272,128]{1,0:T(8,128)(2,1)}, bf16[272,128]{1,0:T(8,128)(2,1)S(1)}, u32[]{:S(2)}, u32[]{:S(2)}) collective-permute-start(bf16[272,128]{1,0:T(8,128)(2,1)} %get-tuple-element.19), channel_id=1, source_target_pairs={{0,24},{1,25},{2,26},{3,27},{4,28},{5,29},{6,30},{7,31},{8,0},{9,1... | collective-permute-start | bytes 208904 | tf_op jit(solution)/shard_map/ppermute | solution.py:223
  12.2 0.0 collective-permute-done.1.refs_2_
  12.2 1.8 %collective-permute-start.6 = (bf16[272,128]{1,0:T(8,128)(2,1)}, bf16[272,128]{1,0:T(8,128)(2,1)S(1)}, u32[]{:S(2)}, u32[]{:S(2)}) collective-permute-start(bf16[272,128]{1,0:T(8,128)(2,1)} %get-tuple-element.20), channel_id=1, source_target_pairs={{0,25},{1,24},{2,27},{3,26},{4,29},{5,28},{6,31},{7,30},{8,1},{9,0... | collective-permute-start | bytes 208904 | tf_op jit(solution)/shard_map/ppermute | solution.py:223
  14.0 10.1 %all-to-all-start = ((bf16[32,32,128]{2,1,0:T(8,128)(2,1)}), bf16[32,32,128]{2,1,0:T(8,128)(2,1)S(1)}, u32[]{:S(2)}, u32[]{:S(2)}) async-start(bf16[32,32,128]{2,1,0:T(8,128)(2,1)} %get-tuple-element.21), calls=%async_computation | async-start | bytes 524288 | tf_op jit(solution)/shard_map/all_to_all | solution.py:245
  24.3 0.0 collective-permute-done.2.refs_3_
  24.3 0.0 collective-permute-done.3.refs_4_
  24.3 0.0 collective-permute-done.4.refs_5_
  24.3 0.0 collective-permute-done.5.refs_6_
  24.3 0.0 collective-permute-done.6.refs_7_
  24.3 0.9 %fusion = bf16[256,128]{1,0:T(8,128)(2,1)S(1)} fusion(bf16[272,128]{1,0:T(8,128)(2,1)S(1)} %collective-permute-done.6.refs_7_, bf16[272,128]{1,0:T(8,128)(2,1)S(1)} %collective-permute-done.5.refs_6_, bf16[272,128]{1,0:T(8,128)(2,1)S(1)} %collective-permute-done.4.refs_5_, bf16[272,128]{1,0:T(8,128)(2,1)S(1)} %collective-permute-done.3.refs_4_, ...), kind=kLoop, calls=%fused_computation.2 | loop fusion | flops 491520 | bytes 589832 | tf_op jit(solution)/shard_map/add | solution.py:248
  25.2 6.4 %collective-permute-start.9 = (bf16[256,128]{1,0:T(8,128)(2,1)S(1)}, bf16[256,128]{1,0:T(8,128)(2,1)S(1)}, u32[]{:S(2)}, u32[]{:S(2)}) collective-permute-start(bf16[256,128]{1,0:T(8,128)(2,1)S(1)} %fusion), channel_id=1, source_target_pairs={{0,4},{1,5},{8,12},{9,13},{16,20},{17,21},{24,28},{25,29},{32,36},... | collective-permute-start | bytes 196616 | tf_op jit(solution)/shard_map/ppermute | solution.py:218
  31.6 1.3 %collective-permute-start.8 = (bf16[256,128]{1,0:T(8,128)(2,1)S(1)}, bf16[256,128]{1,0:T(8,128)(2,1)S(1)}, u32[]{:S(2)}, u32[]{:S(2)}) collective-permute-start(bf16[256,128]{1,0:T(8,128)(2,1)S(1)} %fusion), channel_id=1, source_target_pairs={{0,6},{1,7},{8,14},{9,15},{16,22},{17,23},{24,30},{25,31},{32,38},... | collective-permute-start | bytes 196616 | tf_op jit(solution)/shard_map/ppermute | solution.py:218
  32.9 1.3 %collective-permute-start.7 = (bf16[256,128]{1,0:T(8,128)(2,1)S(1)}, bf16[256,128]{1,0:T(8,128)(2,1)S(1)}, u32[]{:S(2)}, u32[]{:S(2)}) collective-permute-start(bf16[256,128]{1,0:T(8,128)(2,1)S(1)} %fusion), channel_id=1, source_target_pairs={{0,2},{1,3},{8,10},{9,11},{16,18},{17,19},{24,26},{25,27},{32,34},... | collective-permute-start | bytes 196616 | tf_op jit(solution)/shard_map/ppermute | solution.py:218
  34.2 0.0 collective-permute-done.9
  34.2 0.9 %collective-permute-done.8 = bf16[256,128]{1,0:T(8,128)(2,1)S(1)} collective-permute-done((bf16[256,128]{1,0:T(8,128)(2,1)S(1)}, bf16[256,128]{1,0:T(8,128)(2,1)S(1)}, u32[]{:S(2)}, u32[]{:S(2)}) %collective-permute-start.8) | collective-permute-done | bytes 65568 | tf_op jit(solution)/shard_map/ppermute | solution.py:218
  35.1 1.0 %collective-permute-done.7 = bf16[256,128]{1,0:T(8,128)(2,1)S(1)} collective-permute-done((bf16[256,128]{1,0:T(8,128)(2,1)S(1)}, bf16[256,128]{1,0:T(8,128)(2,1)S(1)}, u32[]{:S(2)}, u32[]{:S(2)}) %collective-permute-start.7) | collective-permute-done | bytes 65568 | tf_op jit(solution)/shard_map/ppermute | solution.py:218
  36.1 0.0 copy-start
  36.1 1.5 %collective-permute-start.10 = (bf16[256,128]{1,0:T(8,128)(2,1)S(1)}, bf16[256,128]{1,0:T(8,128)(2,1)S(1)}, u32[]{:S(2)}, u32[]{:S(2)}) collective-permute-start(bf16[256,128]{1,0:T(8,128)(2,1)S(1)} %add_add_fusion), channel_id=1, source_target_pairs={{0,1},{1,0},{2,3},{3,2},{4,5},{5,4},{6,7},{7,6},{8,9},{9,8},{10,11... | collective-permute-start | bytes 196616 | tf_op jit(solution)/shard_map/ppermute | solution.py:223
  37.7 0.0 all-to-all-done.refs_8_
  37.7 0.0 copy-start.1
  37.7 0.9 %copy-done.1 = bf16[272,128]{1,0:T(8,128)(2,1)S(1)} copy-done((bf16[272,128]{1,0:T(8,128)(2,1)S(1)}, bf16[272,128]{1,0:T(8,128)(2,1)}, u32[]{:S(2)}) %copy-start.1) | copy-done | bytes 69656
  38.6 2.5 %shard_map.60 = f32[32,40,128]{2,1,0:T(8,128)S(1)} custom-call(s32[1]{0:T(128)} %bitcast.place_ref, bf16[272,128]{1,0:T(8,128)(2,1)S(1)} %copy-done.1, bf16[272,128]{1,0:T(8,128)(2,1)S(1)} %collective-permute-done.refs_1_, bf16[272,128]{1,0:T(8,128)(2,1)S(1)} %collective-permute-done.1.refs_2_, bf16[272,128]{1,0:T(8,128)(2,1)S(1)} %collective-permute-done.2.refs_3_, ...), custom_call_target="tpu_custom_call" | custom-call | flops 536870912 | bytes 2097152 | tf_op jit(solution)/shard_map/pallas_call | solution.py:254
  41.0 0.8 %convert_element_type.15 = f16[32,40,128]{2,1,0:T(8,128)(2,1)} convert(f32[32,40,128]{2,1,0:T(8,128)S(1)} %shard_map.60) | non-fusion elementwise | flops 163840 | bytes 983040 | tf_op jit(solution)/shard_map/convert_element_type | solution.py:262
  41.8 0.0 collective-permute-done.10
  41.9 2.8 %collective-permute-start.13 = (bf16[2,256,128]{2,1,0:T(8,128)(2,1)S(1)}, bf16[2,256,128]{2,1,0:T(8,128)(2,1)S(1)}, u32[]{:S(2)}, u32[]{:S(2)}) collective-permute-start(bf16[2,256,128]{2,1,0:T(8,128)(2,1)S(1)} %pad_maximum_fusion.a0_ref), channel_id=1, source_target_pairs={{0,24},{1,25},{2,26},{3,27},{4,28},{5,29},{6,30},{7,31},{8,0},{9,1... | collective-permute-start | bytes 393224 | tf_op jit(solution)/shard_map/ppermute | solution.py:223
  44.7 0.8 %collective-permute-start.12 = (bf16[2,256,128]{2,1,0:T(8,128)(2,1)S(1)}, bf16[2,256,128]{2,1,0:T(8,128)(2,1)S(1)}, u32[]{:S(2)}, u32[]{:S(2)}) collective-permute-start(bf16[2,256,128]{2,1,0:T(8,128)(2,1)S(1)} %pad_maximum_fusion.a0_ref), channel_id=1, source_target_pairs={{0,16},{1,17},{2,18},{3,19},{4,20},{5,21},{6,22},{7,23},{8,24},{9,... | collective-permute-start | bytes 393224 | tf_op jit(solution)/shard_map/ppermute | solution.py:223
  45.5 0.9 %collective-permute-start.11 = (bf16[2,256,128]{2,1,0:T(8,128)(2,1)S(1)}, bf16[2,256,128]{2,1,0:T(8,128)(2,1)S(1)}, u32[]{:S(2)}, u32[]{:S(2)}) collective-permute-start(bf16[2,256,128]{2,1,0:T(8,128)(2,1)S(1)} %pad_maximum_fusion.a0_ref), channel_id=1, source_target_pairs={{0,8},{1,9},{2,10},{3,11},{4,12},{5,13},{6,14},{7,15},{8,16},{9,17... | collective-permute-start | bytes 393224 | tf_op jit(solution)/shard_map/ppermute | solution.py:223
  46.4 8.0 %all-to-all-start.1 = ((f16[32,40,128]{2,1,0:T(8,128)(2,1)}), f16[32,40,128]{2,1,0:T(8,128)(2,1)S(1)}, u32[]{:S(2)}, u32[]{:S(2)}) async-start(f16[32,40,128]{2,1,0:T(8,128)(2,1)} %convert_element_type.15), calls=%async_computation.1 | async-start | bytes 655360 | tf_op jit(solution)/shard_map/all_to_all | solution.py:266
  54.3 0.0 collective-permute-done.13.a3_ref
  54.3 0.0 collective-permute-done.12.a2_ref
  54.3 0.0 collective-permute-done.11.a1_ref
  54.3 0.0 copy-done
  54.4 7.7 %shard_map.61 = bf16[128,8192]{1,0:T(8,128)(2,1)} custom-call(s32[1]{0:T(128)} %bitcast.place_ref, bf16[128,8192]{1,0:T(8,128)(2,1)} %q_hbm.3, bf16[2,128,1024]{2,1,0:T(8,128)(2,1)S(1)} %copy-done, bf16[2,256,128]{2,1,0:T(8,128)(2,1)S(1)} %pad_maximum_fusion.a0_ref, bf16[2,256,128]{2,1,0:T(8,128)(2,1)S(1)} %collective-permute-done.11.a1_ref, ...), custom_call_target="tpu_custom_call" | custom-call | flops 68719476736 | bytes 16777216 | tf_op jit(solution)/shard_map/pallas_call | solution.py:267
  62.0 4.1 %all-to-all-done.1 = f16[32,40,128]{2,1,0:T(8,128)(2,1)S(1)} async-done(((f16[32,40,128]{2,1,0:T(8,128)(2,1)}), f16[32,40,128]{2,1,0:T(8,128)(2,1)S(1)}, u32[]{:S(2)}, u32[]{:S(2)}) %all-to-all-start.1) | async-done | bytes 327712 | tf_op jit(solution)/shard_map/all_to_all | solution.py:266
  66.2 0.9 %shard_map.62 = bf16[4,8192]{1,0:T(4,128)(2,1)} custom-call(f32[32,40,128]{2,1,0:T(8,128)S(1)} %convert_element_type.16.in_ref), custom_call_target="tpu_custom_call" | custom-call | flops 1048576 | bytes 1048576 | tf_op jit(solution)/shard_map/pallas_call | solution.py:284
  (4 shorter events, 0.1 us)
Async XLA Ops:
  2.8 7.8 %collective-permute-start = (bf16[272,128]{1,0:T(8,128)(2,1)}, bf16[272,128]{1,0:T(8,128)(2,1)S(1)}, u32[]{:S(2)}, u32[]{:S(2)}) collective-permute-start(bf16[272,128]{1,0:T(8,128)(2,1)} %get-tuple-element.14), channel_id=1, source_target_pairs={{0,1},{1,0},{2,3},{3,2},{4,5},{5,4},{6,7},{7,6},{8,9},{9,8},{10,11... | collective-permute-start | bytes 208904 | tf_op jit(solution)/shard_map/ppermute | solution.py:223
  3.0 9.3 %collective-permute-start.1 = (bf16[272,128]{1,0:T(8,128)(2,1)}, bf16[272,128]{1,0:T(8,128)(2,1)S(1)}, u32[]{:S(2)}, u32[]{:S(2)}) collective-permute-start(bf16[272,128]{1,0:T(8,128)(2,1)} %get-tuple-element.15), channel_id=1, source_target_pairs={{0,8},{1,9},{2,10},{3,11},{4,12},{5,13},{6,14},{7,15},{8,16},{9,17... | collective-permute-start | bytes 208904 | tf_op jit(solution)/shard_map/ppermute | solution.py:223
  4.6 19.7 %collective-permute-start.2 = (bf16[272,128]{1,0:T(8,128)(2,1)}, bf16[272,128]{1,0:T(8,128)(2,1)S(1)}, u32[]{:S(2)}, u32[]{:S(2)}) collective-permute-start(bf16[272,128]{1,0:T(8,128)(2,1)} %get-tuple-element.16), channel_id=1, source_target_pairs={{0,9},{1,8},{2,11},{3,10},{4,13},{5,12},{6,15},{7,14},{8,17},{9,16... | collective-permute-start | bytes 208904 | tf_op jit(solution)/shard_map/ppermute | solution.py:223
  7.5 16.8 %collective-permute-start.3 = (bf16[272,128]{1,0:T(8,128)(2,1)}, bf16[272,128]{1,0:T(8,128)(2,1)S(1)}, u32[]{:S(2)}, u32[]{:S(2)}) collective-permute-start(bf16[272,128]{1,0:T(8,128)(2,1)} %get-tuple-element.17), channel_id=1, source_target_pairs={{0,16},{1,17},{2,18},{3,19},{4,20},{5,21},{6,22},{7,23},{8,24},{9,... | collective-permute-start | bytes 208904 | tf_op jit(solution)/shard_map/ppermute | solution.py:223
  9.0 15.3 %collective-permute-start.4 = (bf16[272,128]{1,0:T(8,128)(2,1)}, bf16[272,128]{1,0:T(8,128)(2,1)S(1)}, u32[]{:S(2)}, u32[]{:S(2)}) collective-permute-start(bf16[272,128]{1,0:T(8,128)(2,1)} %get-tuple-element.18), channel_id=1, source_target_pairs={{0,17},{1,16},{2,19},{3,18},{4,21},{5,20},{6,23},{7,22},{8,25},{9,... | collective-permute-start | bytes 208904 | tf_op jit(solution)/shard_map/ppermute | solution.py:223
  10.6 13.7 %collective-permute-start.5 = (bf16[272,128]{1,0:T(8,128)(2,1)}, bf16[272,128]{1,0:T(8,128)(2,1)S(1)}, u32[]{:S(2)}, u32[]{:S(2)}) collective-permute-start(bf16[272,128]{1,0:T(8,128)(2,1)} %get-tuple-element.19), channel_id=1, source_target_pairs={{0,24},{1,25},{2,26},{3,27},{4,28},{5,29},{6,30},{7,31},{8,0},{9,1... | collective-permute-start | bytes 208904 | tf_op jit(solution)/shard_map/ppermute | solution.py:223
  12.2 12.1 %collective-permute-start.6 = (bf16[272,128]{1,0:T(8,128)(2,1)}, bf16[272,128]{1,0:T(8,128)(2,1)S(1)}, u32[]{:S(2)}, u32[]{:S(2)}) collective-permute-start(bf16[272,128]{1,0:T(8,128)(2,1)} %get-tuple-element.20), channel_id=1, source_target_pairs={{0,25},{1,24},{2,27},{3,26},{4,29},{5,28},{6,31},{7,30},{8,1},{9,0... | collective-permute-start | bytes 208904 | tf_op jit(solution)/shard_map/ppermute | solution.py:223
  14.0 23.6 %all-to-all-start = ((bf16[32,32,128]{2,1,0:T(8,128)(2,1)}), bf16[32,32,128]{2,1,0:T(8,128)(2,1)S(1)}, u32[]{:S(2)}, u32[]{:S(2)}) async-start(bf16[32,32,128]{2,1,0:T(8,128)(2,1)} %get-tuple-element.21), calls=%async_computation | async-start | bytes 524288 | tf_op jit(solution)/shard_map/all_to_all | solution.py:245
  25.2 9.0 %collective-permute-start.9 = (bf16[256,128]{1,0:T(8,128)(2,1)S(1)}, bf16[256,128]{1,0:T(8,128)(2,1)S(1)}, u32[]{:S(2)}, u32[]{:S(2)}) collective-permute-start(bf16[256,128]{1,0:T(8,128)(2,1)S(1)} %fusion), channel_id=1, source_target_pairs={{0,4},{1,5},{8,12},{9,13},{16,20},{17,21},{24,28},{25,29},{32,36},... | collective-permute-start | bytes 196616 | tf_op jit(solution)/shard_map/ppermute | solution.py:218
  31.6 3.5 %collective-permute-start.8 = (bf16[256,128]{1,0:T(8,128)(2,1)S(1)}, bf16[256,128]{1,0:T(8,128)(2,1)S(1)}, u32[]{:S(2)}, u32[]{:S(2)}) collective-permute-start(bf16[256,128]{1,0:T(8,128)(2,1)S(1)} %fusion), channel_id=1, source_target_pairs={{0,6},{1,7},{8,14},{9,15},{16,22},{17,23},{24,30},{25,31},{32,38},... | collective-permute-start | bytes 196616 | tf_op jit(solution)/shard_map/ppermute | solution.py:218
  32.9 3.2 %collective-permute-start.7 = (bf16[256,128]{1,0:T(8,128)(2,1)S(1)}, bf16[256,128]{1,0:T(8,128)(2,1)S(1)}, u32[]{:S(2)}, u32[]{:S(2)}) collective-permute-start(bf16[256,128]{1,0:T(8,128)(2,1)S(1)} %fusion), channel_id=1, source_target_pairs={{0,2},{1,3},{8,10},{9,11},{16,18},{17,19},{24,26},{25,27},{32,34},... | collective-permute-start | bytes 196616 | tf_op jit(solution)/shard_map/ppermute | solution.py:218
  36.1 18.2 %copy-start = (bf16[2,128,1024]{2,1,0:T(8,128)(2,1)S(1)}, bf16[2,128,1024]{2,1,0:T(8,128)(2,1)}, u32[]{:S(2)}) copy-start(bf16[2,128,1024]{2,1,0:T(8,128)(2,1)} %kv_hbm.3) | copy-start | bytes 1572868
  36.1 5.7 %collective-permute-start.10 = (bf16[256,128]{1,0:T(8,128)(2,1)S(1)}, bf16[256,128]{1,0:T(8,128)(2,1)S(1)}, u32[]{:S(2)}, u32[]{:S(2)}) collective-permute-start(bf16[256,128]{1,0:T(8,128)(2,1)S(1)} %add_add_fusion), channel_id=1, source_target_pairs={{0,1},{1,0},{2,3},{3,2},{4,5},{5,4},{6,7},{7,6},{8,9},{9,8},{10,11... | collective-permute-start | bytes 196616 | tf_op jit(solution)/shard_map/ppermute | solution.py:223
  37.7 0.9 %copy-start.1 = (bf16[272,128]{1,0:T(8,128)(2,1)S(1)}, bf16[272,128]{1,0:T(8,128)(2,1)}, u32[]{:S(2)}) copy-start(bf16[272,128]{1,0:T(8,128)(2,1)} %get-tuple-element.13.refs_0_) | copy-start | bytes 208900
  41.9 12.4 %collective-permute-start.13 = (bf16[2,256,128]{2,1,0:T(8,128)(2,1)S(1)}, bf16[2,256,128]{2,1,0:T(8,128)(2,1)S(1)}, u32[]{:S(2)}, u32[]{:S(2)}) collective-permute-start(bf16[2,256,128]{2,1,0:T(8,128)(2,1)S(1)} %pad_maximum_fusion.a0_ref), channel_id=1, source_target_pairs={{0,24},{1,25},{2,26},{3,27},{4,28},{5,29},{6,30},{7,31},{8,0},{9,1... | collective-permute-start | bytes 393224 | tf_op jit(solution)/shard_map/ppermute | solution.py:223
  44.7 9.6 %collective-permute-start.12 = (bf16[2,256,128]{2,1,0:T(8,128)(2,1)S(1)}, bf16[2,256,128]{2,1,0:T(8,128)(2,1)S(1)}, u32[]{:S(2)}, u32[]{:S(2)}) collective-permute-start(bf16[2,256,128]{2,1,0:T(8,128)(2,1)S(1)} %pad_maximum_fusion.a0_ref), channel_id=1, source_target_pairs={{0,16},{1,17},{2,18},{3,19},{4,20},{5,21},{6,22},{7,23},{8,24},{9,... | collective-permute-start | bytes 393224 | tf_op jit(solution)/shard_map/ppermute | solution.py:223
  45.5 8.9 %collective-permute-start.11 = (bf16[2,256,128]{2,1,0:T(8,128)(2,1)S(1)}, bf16[2,256,128]{2,1,0:T(8,128)(2,1)S(1)}, u32[]{:S(2)}, u32[]{:S(2)}) collective-permute-start(bf16[2,256,128]{2,1,0:T(8,128)(2,1)S(1)} %pad_maximum_fusion.a0_ref), channel_id=1, source_target_pairs={{0,8},{1,9},{2,10},{3,11},{4,12},{5,13},{6,14},{7,15},{8,16},{9,17... | collective-permute-start | bytes 393224 | tf_op jit(solution)/shard_map/ppermute | solution.py:223
  46.4 19.8 %all-to-all-start.1 = ((f16[32,40,128]{2,1,0:T(8,128)(2,1)}), f16[32,40,128]{2,1,0:T(8,128)(2,1)S(1)}, u32[]{:S(2)}, u32[]{:S(2)}) async-start(f16[32,40,128]{2,1,0:T(8,128)(2,1)} %convert_element_type.15), calls=%async_computation.1 | async-start | bytes 655360 | tf_op jit(solution)/shard_map/all_to_all | solution.py:266

commit v5 on v4

--- a/solution.py
+++ b/solution.py
@@ -23,6 +23,7 @@
 LOG2E = 1.4426950408889634
 SCALE = D ** -0.5 * LOG2E
 
+FAR = 2
 STEPS = [(dy, flip) for dy in range(YS) for flip in range(SIDES)]
 A_K, A_V, A_SK, A_SV = 0, BLOCK, 2 * BLOCK, 2 * BLOCK + 8
 A_ROWS = A_SV + 8
@@ -36,6 +37,15 @@
 
 def dot_nn(a, b):
     return lax.dot_general(a, b, (((1,), (0,)), ((), ())), preferred_element_type=F32)
+
+
+def side_of(place):
+    return (place + jnp.where(place // SIDES % PAIRS == FAR, 1, 0)) % SIDES
+
+
+def place_of(y, pair, side):
+    swapped = (side + (pair == FAR)) % SIDES
+    return y * (PAIRS * SIDES) + pair * SIDES + swapped
 
 
 def pack_kernel(place_ref, kv_hbm, q_hbm, qkv_hbm, *refs):
@@ -55,8 +65,8 @@
             [q[:, first + j * D:first + (j + 1) * D] for j in range(GROUP)], 0
         ).astype(BF16)
         for pair in range(PAIRS):
-            q_out_ref[head // SIDES * PAIRS * SIDES + pair * SIDES + head % SIDES] = queries
-    y, side = place_ref[0] // (PAIRS * SIDES), place_ref[0] % SIDES
+            q_out_ref[place_of(head // SIDES, pair, head % SIDES)] = queries
+    y, side = place_ref[0] // (PAIRS * SIDES), side_of(place_ref[0])
     blank = jnp.zeros((8 - ROWS, D), F32)
     for (dy, flip), out_ref in zip(STEPS, kv_out_refs):
         head = (y + dy) % YS * SIDES + (side + flip) % SIDES
@@ -75,7 +85,7 @@
 def query_kernel(place_ref, *refs):
     kv_refs, (q_ref, out_ref) = refs[:KV_HEADS], refs[KV_HEADS:]
     place = place_ref[0]
-    y, pair, side = place // (PAIRS * SIDES), place // SIDES % PAIRS, place % SIDES
+    y, pair, side = place // (PAIRS * SIDES), place // SIDES % PAIRS, side_of(place)
     keys = jnp.concatenate([ref[A_K:A_K + BLOCK, :] for ref in kv_refs], 0)
     values = jnp.concatenate([ref[A_V:A_V + BLOCK, :] for ref in kv_refs], 0)
     tails = [ref[A_SK:A_ROWS, :].astype(F32) for ref in kv_refs]
@@ -86,6 +96,7 @@
     column = lax.broadcasted_iota(jnp.int32, (rows, KV_HEADS * 8), 1)
     source, key_row = column // 8, column % 8
     source_y, source_side = (y + YS - source // SIDES) % YS, (side + source % SIDES) % SIDES
+    source_side = (source_side + jnp.where(pair == FAR, 1, 0)) % SIDES
     key_pos = (source_y * (PAIRS * SIDES) + pair * SIDES + source_side) * ROWS + key_row
     key_pos = jnp.where(key_row < ROWS, key_pos, CTX * ROWS)
     row_pos = (row_id // QROWS) * ROWS + row_id % ROWS
@@ -176,9 +187,11 @@
         == lax.broadcasted_iota(jnp.int32, (KV_HEADS, QROWS, D), 2)
     )
     received = in_ref[...].reshape(YS, PAIRS, SIDES, B_ROWS, D)
+    received = [received[:, pair] for pair in range(PAIRS)]
+    received[FAR] = jnp.concatenate([received[FAR][:, 1:2], received[FAR][:, 0:1]], 1)
     logs = []
     for pair in range(PAIRS):
-        parts = received[:, pair, :, B_S:, :].reshape(KV_HEADS, B_ROWS - B_S, D)
+        parts = received[pair][:, :, B_S:, :].reshape(KV_HEADS, B_ROWS - B_S, D)
         logs.append(parts[:, 0:1, :] + parts[:, 1:2, :] + parts[:, 2:3, :])
     highest = functools.reduce(jnp.maximum, logs)
     shares = [jnp.exp2(log - highest) for log in logs]
@@ -186,7 +199,7 @@
     merged = jnp.zeros((KV_HEADS, QROWS, D), F32)
     for pair in range(PAIRS):
         share = jnp.sum(jnp.where(diagonal, shares[pair] / whole, 0.0), 2, keepdims=True)
-        merged = merged + share * received[:, pair, :, 0:QROWS, :].reshape(KV_HEADS, QROWS, D)
+        merged = merged + share * received[pair][:, :, 0:QROWS, :].reshape(KV_HEADS, QROWS, D)
     for head in range(KV_HEADS):
         for j in range(GROUP):
             first = (head * GROUP + j) * D
@@ -213,8 +226,8 @@
 
 def fan_along_z(piece):
     result = piece
-    for step in (2, 6, 4):
-        pairs = [(at(y, side), at(y, side + step)) for y in range(YS) for side in range(SIDES)]
+    for pair in (1, 3, FAR):
+        pairs = [(place_of(y, 0, side), place_of(y, pair, side)) for y in range(YS) for side in range(SIDES)]
         result = result + lax.ppermute(piece, "ctx", pairs)
     return result
 
@@ -226,7 +239,7 @@
 def per_device(context_q, context_key_value, query_token_queries, query_key_value):
     index = lax.axis_index("ctx")
     place = index.astype(jnp.int32).reshape(1)
-    y, side = index // (PAIRS * SIDES), index % SIDES
+    y, side = index // (PAIRS * SIDES), side_of(index)
     *packed_kv, packed_q = pl.pallas_call(
         pack_kernel,
         out_shape=(jax.ShapeDtypeStruct((A_ROWS, D), BF16),) * KV_HEADS

time: 67.5 us -> 67.3 us (level)
    ppermute x11, starting transfers between devices: 17.3 us -> 16.4 us  [step_in_pair(): lax.ppermute(array, 'ctx', [(at(y, z), at((y + dy) % YS, z ^ flip)) for y...]
where the time goes in v5:
time: 67.3 us; the launch traced here: 66.9 us
  starting transfers between devices  43.7 us (65%)
  Pallas kernels  13.2 us (20%)
  waiting for transfers between devices  6.45 us (10%)
  other arithmetic  1.77 us (3%)
  local copies, waits for them, and re-layouts  0.89 us (1%)
  between operations  0.89 us (1%)
    ppermute x11, starting transfers between devices, step_in_pair(): lax.ppermute(array, 'ctx', [(at(y, z), at((y + dy) % YS, z ^ flip)) for y...  16.4 us
    all_to_all x1, starting transfers between devices, per_device(): queries = lax.all_to_all(packed_q, 'ctx', 0, 0)  10.1 us
    ppermute x3, starting transfers between devices, fan_along_z(): result = result + lax.ppermute(piece, 'ctx', pairs)  8.97 us
    all_to_all x1, starting transfers between devices, per_device(): gathered = lax.all_to_all(halved, 'ctx', 0, 0).astype(F32)  8.18 us
    pallas_call x1, Pallas kernels, per_device(): pl.pallas_call(encode_kernel, out_shape=jax.ShapeDtypeStruct(context_q.sh...  7.68 us
    all_to_all x1, waiting for transfers between devices, per_device(): gathered = lax.all_to_all(halved, 'ctx', 0, 0).astype(F32)  4.11 us
    pallas_call x1, Pallas kernels, per_device(): pl.pallas_call(query_kernel, out_shape=jax.ShapeDtypeStruct((CTX, B_ROWS,...  2.47 us
    ppermute x3, waiting for transfers between devices, fan_along_z(): result = result + lax.ppermute(piece, 'ctx', pairs)  2.31 us
  transfers between devices with their start and end apart: 16, of which 3 were waited for; matrix products, arithmetic and copies ran while one was open for 3% of the time, Pallas kernels for 15%

profile of v5, /device:TPU:36, one launch (start us, length us, event | category | flops | bytes accessed | tf_op | source)
XLA Modules:
  0.0 66.9 jit_solution(14949879813666943259)
XLA Ops:
  0.6 2.2 %shard_map.59 = (bf16[272,128]{1,0:T(8,128)(2,1)}, bf16[272,128]{1,0:T(8,128)(2,1)}, bf16[272,128]{1,0:T(8,128)(2,1)}, bf16[272,128]{1,0:T(8,128)(2,1)}, bf16[27...) custom-call(s32[1]{0:T(128)} %bitcast.place_ref, ...), custom_call_target="tpu_custom_call" | custom-call | bytes 2097152 | tf_op jit(solution)/shard_map/pallas_call | solution.py:243
  2.8 0.2 collective-permute-start
  3.0 1.6 %collective-permute-start.1 = (bf16[272,128]{1,0:T(8,128)(2,1)}, bf16[272,128]{1,0:T(8,128)(2,1)S(1)}, u32[]{:S(2)}, u32[]{:S(2)}) collective-permute-start(bf16[272,128]{1,0:T(8,128)(2,1)} %get-tuple-element.15), channel_id=1, source_target_pairs={{0,8},{1,9},{2,10},{3,11},{4,12},{5,13},{6,14},{7,15},{8,16},{9,17... | collective-permute-start | bytes 208904 | tf_op jit(solution)/shard_map/ppermute | solution.py:236
  4.6 2.9 %collective-permute-start.2 = (bf16[272,128]{1,0:T(8,128)(2,1)}, bf16[272,128]{1,0:T(8,128)(2,1)S(1)}, u32[]{:S(2)}, u32[]{:S(2)}) collective-permute-start(bf16[272,128]{1,0:T(8,128)(2,1)} %get-tuple-element.16), channel_id=1, source_target_pairs={{0,9},{1,8},{2,11},{3,10},{4,13},{5,12},{6,15},{7,14},{8,17},{9,16... | collective-permute-start | bytes 208904 | tf_op jit(solution)/shard_map/ppermute | solution.py:236
  7.5 1.5 %collective-permute-start.3 = (bf16[272,128]{1,0:T(8,128)(2,1)}, bf16[272,128]{1,0:T(8,128)(2,1)S(1)}, u32[]{:S(2)}, u32[]{:S(2)}) collective-permute-start(bf16[272,128]{1,0:T(8,128)(2,1)} %get-tuple-element.17), channel_id=1, source_target_pairs={{0,16},{1,17},{2,18},{3,19},{4,20},{5,21},{6,22},{7,23},{8,24},{9,... | collective-permute-start | bytes 208904 | tf_op jit(solution)/shard_map/ppermute | solution.py:236
  9.0 1.5 %collective-permute-start.4 = (bf16[272,128]{1,0:T(8,128)(2,1)}, bf16[272,128]{1,0:T(8,128)(2,1)S(1)}, u32[]{:S(2)}, u32[]{:S(2)}) collective-permute-start(bf16[272,128]{1,0:T(8,128)(2,1)} %get-tuple-element.18), channel_id=1, source_target_pairs={{0,17},{1,16},{2,19},{3,18},{4,21},{5,20},{6,23},{7,22},{8,25},{9,... | collective-permute-start | bytes 208904 | tf_op jit(solution)/shard_map/ppermute | solution.py:236
  10.6 0.0 collective-permute-done.refs_1_
  10.6 1.7 %collective-permute-start.5 = (bf16[272,128]{1,0:T(8,128)(2,1)}, bf16[272,128]{1,0:T(8,128)(2,1)S(1)}, u32[]{:S(2)}, u32[]{:S(2)}) collective-permute-start(bf16[272,128]{1,0:T(8,128)(2,1)} %get-tuple-element.19), channel_id=1, source_target_pairs={{0,24},{1,25},{2,26},{3,27},{4,28},{5,29},{6,30},{7,31},{8,0},{9,1... | collective-permute-start | bytes 208904 | tf_op jit(solution)/shard_map/ppermute | solution.py:236
  12.2 0.0 collective-permute-done.1.refs_2_
  12.2 1.8 %collective-permute-start.6 = (bf16[272,128]{1,0:T(8,128)(2,1)}, bf16[272,128]{1,0:T(8,128)(2,1)S(1)}, u32[]{:S(2)}, u32[]{:S(2)}) collective-permute-start(bf16[272,128]{1,0:T(8,128)(2,1)} %get-tuple-element.20), channel_id=1, source_target_pairs={{0,25},{1,24},{2,27},{3,26},{4,29},{5,28},{6,31},{7,30},{8,1},{9,0... | collective-permute-start | bytes 208904 | tf_op jit(solution)/shard_map/ppermute | solution.py:236
  14.0 10.1 %all-to-all-start = ((bf16[32,32,128]{2,1,0:T(8,128)(2,1)}), bf16[32,32,128]{2,1,0:T(8,128)(2,1)S(1)}, u32[]{:S(2)}, u32[]{:S(2)}) async-start(bf16[32,32,128]{2,1,0:T(8,128)(2,1)} %get-tuple-element.21), calls=%async_computation | async-start | bytes 524288 | tf_op jit(solution)/shard_map/all_to_all | solution.py:258
  24.3 0.0 collective-permute-done.2.refs_3_
  24.3 0.0 collective-permute-done.3.refs_4_
  24.3 0.0 collective-permute-done.4.refs_5_
  24.3 0.0 collective-permute-done.5.refs_6_
  24.3 0.0 collective-permute-done.6.refs_7_
  24.3 0.9 %fusion = bf16[256,128]{1,0:T(8,128)(2,1)S(1)} fusion(bf16[272,128]{1,0:T(8,128)(2,1)S(1)} %collective-permute-done.6.refs_7_, bf16[272,128]{1,0:T(8,128)(2,1)S(1)} %collective-permute-done.5.refs_6_, bf16[272,128]{1,0:T(8,128)(2,1)S(1)} %collective-permute-done.4.refs_5_, bf16[272,128]{1,0:T(8,128)(2,1)S(1)} %collective-permute-done.3.refs_4_, ...), kind=kLoop, calls=%fused_computation.2 | loop fusion | flops 491520 | bytes 589832 | tf_op jit(solution)/shard_map/add | solution.py:261
  25.2 6.4 %collective-permute-start.9 = (bf16[256,128]{1,0:T(8,128)(2,1)S(1)}, bf16[256,128]{1,0:T(8,128)(2,1)S(1)}, u32[]{:S(2)}, u32[]{:S(2)}) collective-permute-start(bf16[256,128]{1,0:T(8,128)(2,1)S(1)} %fusion), channel_id=1, source_target_pairs={{0,5},{1,4},{8,13},{9,12},{16,21},{17,20},{24,29},{25,28},{32,37},... | collective-permute-start | bytes 196616 | tf_op jit(solution)/shard_map/ppermute | solution.py:231
  31.6 1.3 %collective-permute-start.8 = (bf16[256,128]{1,0:T(8,128)(2,1)S(1)}, bf16[256,128]{1,0:T(8,128)(2,1)S(1)}, u32[]{:S(2)}, u32[]{:S(2)}) collective-permute-start(bf16[256,128]{1,0:T(8,128)(2,1)S(1)} %fusion), channel_id=1, source_target_pairs={{0,6},{1,7},{8,14},{9,15},{16,22},{17,23},{24,30},{25,31},{32,38},... | collective-permute-start | bytes 196616 | tf_op jit(solution)/shard_map/ppermute | solution.py:231
  32.9 1.3 %collective-permute-start.7 = (bf16[256,128]{1,0:T(8,128)(2,1)S(1)}, bf16[256,128]{1,0:T(8,128)(2,1)S(1)}, u32[]{:S(2)}, u32[]{:S(2)}) collective-permute-start(bf16[256,128]{1,0:T(8,128)(2,1)S(1)} %fusion), channel_id=1, source_target_pairs={{0,2},{1,3},{8,10},{9,11},{16,18},{17,19},{24,26},{25,27},{32,34},... | collective-permute-start | bytes 196616 | tf_op jit(solution)/shard_map/ppermute | solution.py:231
  34.2 0.0 collective-permute-done.9
  34.2 1.1 %collective-permute-done.8 = bf16[256,128]{1,0:T(8,128)(2,1)S(1)} collective-permute-done((bf16[256,128]{1,0:T(8,128)(2,1)S(1)}, bf16[256,128]{1,0:T(8,128)(2,1)S(1)}, u32[]{:S(2)}, u32[]{:S(2)}) %collective-permute-start.8) | collective-permute-done | bytes 65568 | tf_op jit(solution)/shard_map/ppermute | solution.py:231
  35.4 1.2 %collective-permute-done.7 = bf16[256,128]{1,0:T(8,128)(2,1)S(1)} collective-permute-done((bf16[256,128]{1,0:T(8,128)(2,1)S(1)}, bf16[256,128]{1,0:T(8,128)(2,1)S(1)}, u32[]{:S(2)}, u32[]{:S(2)}) %collective-permute-start.7) | collective-permute-done | bytes 65568 | tf_op jit(solution)/shard_map/ppermute | solution.py:231
  36.6 0.0 copy-start
  36.6 0.7 %collective-permute-start.10 = (bf16[256,128]{1,0:T(8,128)(2,1)S(1)}, bf16[256,128]{1,0:T(8,128)(2,1)S(1)}, u32[]{:S(2)}, u32[]{:S(2)}) collective-permute-start(bf16[256,128]{1,0:T(8,128)(2,1)S(1)} %add_add_fusion), channel_id=1, source_target_pairs={{0,1},{1,0},{2,3},{3,2},{4,5},{5,4},{6,7},{7,6},{8,9},{9,8},{10,11... | collective-permute-start | bytes 196616 | tf_op jit(solution)/shard_map/ppermute | solution.py:236
  37.3 0.0 all-to-all-done.refs_8_
  37.3 0.0 copy-start.1
  37.3 0.9 %copy-done.1 = bf16[272,128]{1,0:T(8,128)(2,1)S(1)} copy-done((bf16[272,128]{1,0:T(8,128)(2,1)S(1)}, bf16[272,128]{1,0:T(8,128)(2,1)}, u32[]{:S(2)}) %copy-start.1) | copy-done | bytes 69656
  38.2 2.5 %shard_map.60 = f32[32,40,128]{2,1,0:T(8,128)S(1)} custom-call(s32[1]{0:T(128)} %bitcast.place_ref, bf16[272,128]{1,0:T(8,128)(2,1)S(1)} %copy-done.1, bf16[272,128]{1,0:T(8,128)(2,1)S(1)} %collective-permute-done.refs_1_, bf16[272,128]{1,0:T(8,128)(2,1)S(1)} %collective-permute-done.1.refs_2_, bf16[272,128]{1,0:T(8,128)(2,1)S(1)} %collective-permute-done.2.refs_3_, ...), custom_call_target="tpu_custom_call" | custom-call | flops 536870912 | bytes 2097152 | tf_op jit(solution)/shard_map/pallas_call | solution.py:267
  40.6 0.8 %convert_element_type.15 = f16[32,40,128]{2,1,0:T(8,128)(2,1)} convert(f32[32,40,128]{2,1,0:T(8,128)S(1)} %shard_map.60) | non-fusion elementwise | flops 163840 | bytes 983040 | tf_op jit(solution)/shard_map/convert_element_type | solution.py:275
  41.4 0.0 collective-permute-done.10
  41.5 2.8 %collective-permute-start.13 = (bf16[2,256,128]{2,1,0:T(8,128)(2,1)S(1)}, bf16[2,256,128]{2,1,0:T(8,128)(2,1)S(1)}, u32[]{:S(2)}, u32[]{:S(2)}) collective-permute-start(bf16[2,256,128]{2,1,0:T(8,128)(2,1)S(1)} %pad_maximum_fusion.a0_ref), channel_id=1, source_target_pairs={{0,24},{1,25},{2,26},{3,27},{4,28},{5,29},{6,30},{7,31},{8,0},{9,1... | collective-permute-start | bytes 393224 | tf_op jit(solution)/shard_map/ppermute | solution.py:236
  44.3 0.8 %collective-permute-start.12 = (bf16[2,256,128]{2,1,0:T(8,128)(2,1)S(1)}, bf16[2,256,128]{2,1,0:T(8,128)(2,1)S(1)}, u32[]{:S(2)}, u32[]{:S(2)}) collective-permute-start(bf16[2,256,128]{2,1,0:T(8,128)(2,1)S(1)} %pad_maximum_fusion.a0_ref), channel_id=1, source_target_pairs={{0,16},{1,17},{2,18},{3,19},{4,20},{5,21},{6,22},{7,23},{8,24},{9,... | collective-permute-start | bytes 393224 | tf_op jit(solution)/shard_map/ppermute | solution.py:236
  45.1 0.9 %collective-permute-start.11 = (bf16[2,256,128]{2,1,0:T(8,128)(2,1)S(1)}, bf16[2,256,128]{2,1,0:T(8,128)(2,1)S(1)}, u32[]{:S(2)}, u32[]{:S(2)}) collective-permute-start(bf16[2,256,128]{2,1,0:T(8,128)(2,1)S(1)} %pad_maximum_fusion.a0_ref), channel_id=1, source_target_pairs={{0,8},{1,9},{2,10},{3,11},{4,12},{5,13},{6,14},{7,15},{8,16},{9,17... | collective-permute-start | bytes 393224 | tf_op jit(solution)/shard_map/ppermute | solution.py:236
  46.0 8.2 %all-to-all-start.1 = ((f16[32,40,128]{2,1,0:T(8,128)(2,1)}), f16[32,40,128]{2,1,0:T(8,128)(2,1)S(1)}, u32[]{:S(2)}, u32[]{:S(2)}) async-start(f16[32,40,128]{2,1,0:T(8,128)(2,1)} %convert_element_type.15), calls=%async_computation.1 | async-start | bytes 655360 | tf_op jit(solution)/shard_map/all_to_all | solution.py:279
  54.1 0.0 collective-permute-done.13.a3_ref
  54.2 0.0 collective-permute-done.12.a2_ref
  54.2 0.0 collective-permute-done.11.a1_ref
  54.2 0.0 copy-done
  54.2 7.7 %shard_map.61 = bf16[128,8192]{1,0:T(8,128)(2,1)} custom-call(s32[1]{0:T(128)} %bitcast.place_ref, bf16[128,8192]{1,0:T(8,128)(2,1)} %q_hbm.3, bf16[2,128,1024]{2,1,0:T(8,128)(2,1)S(1)} %copy-done, bf16[2,256,128]{2,1,0:T(8,128)(2,1)S(1)} %pad_maximum_fusion.a0_ref, bf16[2,256,128]{2,1,0:T(8,128)(2,1)S(1)} %collective-permute-done.11.a1_ref, ...), custom_call_target="tpu_custom_call" | custom-call | flops 68719476736 | bytes 16777216 | tf_op jit(solution)/shard_map/pallas_call | solution.py:280
  61.9 4.1 %all-to-all-done.1 = f16[32,40,128]{2,1,0:T(8,128)(2,1)S(1)} async-done(((f16[32,40,128]{2,1,0:T(8,128)(2,1)}), f16[32,40,128]{2,1,0:T(8,128)(2,1)S(1)}, u32[]{:S(2)}, u32[]{:S(2)}) %all-to-all-start.1) | async-done | bytes 327712 | tf_op jit(solution)/shard_map/all_to_all | solution.py:279
  66.0 0.9 %shard_map.62 = bf16[4,8192]{1,0:T(4,128)(2,1)} custom-call(f32[32,40,128]{2,1,0:T(8,128)S(1)} %convert_element_type.16.in_ref), custom_call_target="tpu_custom_call" | custom-call | flops 1048576 | bytes 1048576 | tf_op jit(solution)/shard_map/pallas_call | solution.py:297
  (4 shorter events, 0.1 us)
Async XLA Ops:
  2.8 7.8 %collective-permute-start = (bf16[272,128]{1,0:T(8,128)(2,1)}, bf16[272,128]{1,0:T(8,128)(2,1)S(1)}, u32[]{:S(2)}, u32[]{:S(2)}) collective-permute-start(bf16[272,128]{1,0:T(8,128)(2,1)} %get-tuple-element.14), channel_id=1, source_target_pairs={{0,1},{1,0},{2,3},{3,2},{4,5},{5,4},{6,7},{7,6},{8,9},{9,8},{10,11... | collective-permute-start | bytes 208904 | tf_op jit(solution)/shard_map/ppermute | solution.py:236
  3.0 9.3 %collective-permute-start.1 = (bf16[272,128]{1,0:T(8,128)(2,1)}, bf16[272,128]{1,0:T(8,128)(2,1)S(1)}, u32[]{:S(2)}, u32[]{:S(2)}) collective-permute-start(bf16[272,128]{1,0:T(8,128)(2,1)} %get-tuple-element.15), channel_id=1, source_target_pairs={{0,8},{1,9},{2,10},{3,11},{4,12},{5,13},{6,14},{7,15},{8,16},{9,17... | collective-permute-start | bytes 208904 | tf_op jit(solution)/shard_map/ppermute | solution.py:236
  4.6 19.7 %collective-permute-start.2 = (bf16[272,128]{1,0:T(8,128)(2,1)}, bf16[272,128]{1,0:T(8,128)(2,1)S(1)}, u32[]{:S(2)}, u32[]{:S(2)}) collective-permute-start(bf16[272,128]{1,0:T(8,128)(2,1)} %get-tuple-element.16), channel_id=1, source_target_pairs={{0,9},{1,8},{2,11},{3,10},{4,13},{5,12},{6,15},{7,14},{8,17},{9,16... | collective-permute-start | bytes 208904 | tf_op jit(solution)/shard_map/ppermute | solution.py:236
  7.5 16.8 %collective-permute-start.3 = (bf16[272,128]{1,0:T(8,128)(2,1)}, bf16[272,128]{1,0:T(8,128)(2,1)S(1)}, u32[]{:S(2)}, u32[]{:S(2)}) collective-permute-start(bf16[272,128]{1,0:T(8,128)(2,1)} %get-tuple-element.17), channel_id=1, source_target_pairs={{0,16},{1,17},{2,18},{3,19},{4,20},{5,21},{6,22},{7,23},{8,24},{9,... | collective-permute-start | bytes 208904 | tf_op jit(solution)/shard_map/ppermute | solution.py:236
  9.0 15.3 %collective-permute-start.4 = (bf16[272,128]{1,0:T(8,128)(2,1)}, bf16[272,128]{1,0:T(8,128)(2,1)S(1)}, u32[]{:S(2)}, u32[]{:S(2)}) collective-permute-start(bf16[272,128]{1,0:T(8,128)(2,1)} %get-tuple-element.18), channel_id=1, source_target_pairs={{0,17},{1,16},{2,19},{3,18},{4,21},{5,20},{6,23},{7,22},{8,25},{9,... | collective-permute-start | bytes 208904 | tf_op jit(solution)/shard_map/ppermute | solution.py:236
  10.6 13.7 %collective-permute-start.5 = (bf16[272,128]{1,0:T(8,128)(2,1)}, bf16[272,128]{1,0:T(8,128)(2,1)S(1)}, u32[]{:S(2)}, u32[]{:S(2)}) collective-permute-start(bf16[272,128]{1,0:T(8,128)(2,1)} %get-tuple-element.19), channel_id=1, source_target_pairs={{0,24},{1,25},{2,26},{3,27},{4,28},{5,29},{6,30},{7,31},{8,0},{9,1... | collective-permute-start | bytes 208904 | tf_op jit(solution)/shard_map/ppermute | solution.py:236
  12.2 12.1 %collective-permute-start.6 = (bf16[272,128]{1,0:T(8,128)(2,1)}, bf16[272,128]{1,0:T(8,128)(2,1)S(1)}, u32[]{:S(2)}, u32[]{:S(2)}) collective-permute-start(bf16[272,128]{1,0:T(8,128)(2,1)} %get-tuple-element.20), channel_id=1, source_target_pairs={{0,25},{1,24},{2,27},{3,26},{4,29},{5,28},{6,31},{7,30},{8,1},{9,0... | collective-permute-start | bytes 208904 | tf_op jit(solution)/shard_map/ppermute | solution.py:236
  14.0 23.2 %all-to-all-start = ((bf16[32,32,128]{2,1,0:T(8,128)(2,1)}), bf16[32,32,128]{2,1,0:T(8,128)(2,1)S(1)}, u32[]{:S(2)}, u32[]{:S(2)}) async-start(bf16[32,32,128]{2,1,0:T(8,128)(2,1)} %get-tuple-element.21), calls=%async_computation | async-start | bytes 524288 | tf_op jit(solution)/shard_map/all_to_all | solution.py:258
  25.2 9.0 %collective-permute-start.9 = (bf16[256,128]{1,0:T(8,128)(2,1)S(1)}, bf16[256,128]{1,0:T(8,128)(2,1)S(1)}, u32[]{:S(2)}, u32[]{:S(2)}) collective-permute-start(bf16[256,128]{1,0:T(8,128)(2,1)S(1)} %fusion), channel_id=1, source_target_pairs={{0,5},{1,4},{8,13},{9,12},{16,21},{17,20},{24,29},{25,28},{32,37},... | collective-permute-start | bytes 196616 | tf_op jit(solution)/shard_map/ppermute | solution.py:231
  31.6 3.7 %collective-permute-start.8 = (bf16[256,128]{1,0:T(8,128)(2,1)S(1)}, bf16[256,128]{1,0:T(8,128)(2,1)S(1)}, u32[]{:S(2)}, u32[]{:S(2)}) collective-permute-start(bf16[256,128]{1,0:T(8,128)(2,1)S(1)} %fusion), channel_id=1, source_target_pairs={{0,6},{1,7},{8,14},{9,15},{16,22},{17,23},{24,30},{25,31},{32,38},... | collective-permute-start | bytes 196616 | tf_op jit(solution)/shard_map/ppermute | solution.py:231
  32.9 3.6 %collective-permute-start.7 = (bf16[256,128]{1,0:T(8,128)(2,1)S(1)}, bf16[256,128]{1,0:T(8,128)(2,1)S(1)}, u32[]{:S(2)}, u32[]{:S(2)}) collective-permute-start(bf16[256,128]{1,0:T(8,128)(2,1)S(1)} %fusion), channel_id=1, source_target_pairs={{0,2},{1,3},{8,10},{9,11},{16,18},{17,19},{24,26},{25,27},{32,34},... | collective-permute-start | bytes 196616 | tf_op jit(solution)/shard_map/ppermute | solution.py:231
  36.6 17.6 %copy-start = (bf16[2,128,1024]{2,1,0:T(8,128)(2,1)S(1)}, bf16[2,128,1024]{2,1,0:T(8,128)(2,1)}, u32[]{:S(2)}) copy-start(bf16[2,128,1024]{2,1,0:T(8,128)(2,1)} %kv_hbm.3) | copy-start | bytes 1572868
  36.6 4.8 %collective-permute-start.10 = (bf16[256,128]{1,0:T(8,128)(2,1)S(1)}, bf16[256,128]{1,0:T(8,128)(2,1)S(1)}, u32[]{:S(2)}, u32[]{:S(2)}) collective-permute-start(bf16[256,128]{1,0:T(8,128)(2,1)S(1)} %add_add_fusion), channel_id=1, source_target_pairs={{0,1},{1,0},{2,3},{3,2},{4,5},{5,4},{6,7},{7,6},{8,9},{9,8},{10,11... | collective-permute-start | bytes 196616 | tf_op jit(solution)/shard_map/ppermute | solution.py:236
  37.3 0.9 %copy-start.1 = (bf16[272,128]{1,0:T(8,128)(2,1)S(1)}, bf16[272,128]{1,0:T(8,128)(2,1)}, u32[]{:S(2)}) copy-start(bf16[272,128]{1,0:T(8,128)(2,1)} %get-tuple-element.13.refs_0_) | copy-start | bytes 208900
  41.5 12.7 %collective-permute-start.13 = (bf16[2,256,128]{2,1,0:T(8,128)(2,1)S(1)}, bf16[2,256,128]{2,1,0:T(8,128)(2,1)S(1)}, u32[]{:S(2)}, u32[]{:S(2)}) collective-permute-start(bf16[2,256,128]{2,1,0:T(8,128)(2,1)S(1)} %pad_maximum_fusion.a0_ref), channel_id=1, source_target_pairs={{0,24},{1,25},{2,26},{3,27},{4,28},{5,29},{6,30},{7,31},{8,0},{9,1... | collective-permute-start | bytes 393224 | tf_op jit(solution)/shard_map/ppermute | solution.py:236
  44.3 9.9 %collective-permute-start.12 = (bf16[2,256,128]{2,1,0:T(8,128)(2,1)S(1)}, bf16[2,256,128]{2,1,0:T(8,128)(2,1)S(1)}, u32[]{:S(2)}, u32[]{:S(2)}) collective-permute-start(bf16[2,256,128]{2,1,0:T(8,128)(2,1)S(1)} %pad_maximum_fusion.a0_ref), channel_id=1, source_target_pairs={{0,16},{1,17},{2,18},{3,19},{4,20},{5,21},{6,22},{7,23},{8,24},{9,... | collective-permute-start | bytes 393224 | tf_op jit(solution)/shard_map/ppermute | solution.py:236
  45.1 9.1 %collective-permute-start.11 = (bf16[2,256,128]{2,1,0:T(8,128)(2,1)S(1)}, bf16[2,256,128]{2,1,0:T(8,128)(2,1)S(1)}, u32[]{:S(2)}, u32[]{:S(2)}) collective-permute-start(bf16[2,256,128]{2,1,0:T(8,128)(2,1)S(1)} %pad_maximum_fusion.a0_ref), channel_id=1, source_target_pairs={{0,8},{1,9},{2,10},{3,11},{4,12},{5,13},{6,14},{7,15},{8,16},{9,17... | collective-permute-start | bytes 393224 | tf_op jit(solution)/shard_map/ppermute | solution.py:236
  46.0 20.0 %all-to-all-start.1 = ((f16[32,40,128]{2,1,0:T(8,128)(2,1)}), f16[32,40,128]{2,1,0:T(8,128)(2,1)S(1)}, u32[]{:S(2)}, u32[]{:S(2)}) async-start(f16[32,40,128]{2,1,0:T(8,128)(2,1)} %convert_element_type.15), calls=%async_computation.1 | async-start | bytes 655360 | tf_op jit(solution)/shard_map/all_to_all | solution.py:279

commit v6 on v5

--- a/solution.py
+++ b/solution.py
@@ -78,7 +78,7 @@
         ).astype(BF16)
 
 
-CHUNK = 8
+CHUNK = 16
 STACK = 4
 
 

time: 67.3 us -> 67.2 us (level)
  no operation moved by 1% of the time
where the time goes in v6:
time: 67.2 us; the launch traced here: 66.7 us
  starting transfers between devices  43.7 us (65%)
  Pallas kernels  13.1 us (19%)
  waiting for transfers between devices  6.35 us (9%)
  other arithmetic  1.77 us (3%)
  local copies, waits for them, and re-layouts  0.89 us (1%)
  between operations  0.89 us (1%)
    ppermute x11, starting transfers between devices, step_in_pair(): lax.ppermute(array, 'ctx', [(at(y, z), at((y + dy) % YS, z ^ flip)) for y...  16.4 us
    all_to_all x1, starting transfers between devices, per_device(): queries = lax.all_to_all(packed_q, 'ctx', 0, 0)  10.1 us
    ppermute x3, starting transfers between devices, fan_along_z(): result = result + lax.ppermute(piece, 'ctx', pairs)  8.97 us
    all_to_all x1, starting transfers between devices, per_device(): gathered = lax.all_to_all(halved, 'ctx', 0, 0).astype(F32)  8.19 us
    pallas_call x1, Pallas kernels, per_device(): pl.pallas_call(encode_kernel, out_shape=jax.ShapeDtypeStruct(context_q.sh...  7.68 us
    all_to_all x1, waiting for transfers between devices, per_device(): gathered = lax.all_to_all(halved, 'ctx', 0, 0).astype(F32)  4.01 us
    pallas_call x1, Pallas kernels, per_device(): pl.pallas_call(query_kernel, out_shape=jax.ShapeDtypeStruct((CTX, B_ROWS,...  2.36 us
    ppermute x3, waiting for transfers between devices, fan_along_z(): result = result + lax.ppermute(piece, 'ctx', pairs)  2.31 us
  transfers between devices with their start and end apart: 16, of which 3 were waited for; matrix products, arithmetic and copies ran while one was open for 3% of the time, Pallas kernels for 15%

profile of v6, /device:TPU:36, one launch (start us, length us, event | category | flops | bytes accessed | tf_op | source)
XLA Modules:
  0.0 66.7 jit_solution(15132976841819072772)
XLA Ops:
  0.6 2.2 %shard_map.59 = (bf16[272,128]{1,0:T(8,128)(2,1)}, bf16[272,128]{1,0:T(8,128)(2,1)}, bf16[272,128]{1,0:T(8,128)(2,1)}, bf16[272,128]{1,0:T(8,128)(2,1)}, bf16[27...) custom-call(s32[1]{0:T(128)} %bitcast.place_ref, ...), custom_call_target="tpu_custom_call" | custom-call | bytes 2097152 | tf_op jit(solution)/shard_map/pallas_call | solution.py:243
  2.8 0.2 collective-permute-start
  3.0 1.6 %collective-permute-start.1 = (bf16[272,128]{1,0:T(8,128)(2,1)}, bf16[272,128]{1,0:T(8,128)(2,1)S(1)}, u32[]{:S(2)}, u32[]{:S(2)}) collective-permute-start(bf16[272,128]{1,0:T(8,128)(2,1)} %get-tuple-element.15), channel_id=1, source_target_pairs={{0,8},{1,9},{2,10},{3,11},{4,12},{5,13},{6,14},{7,15},{8,16},{9,17... | collective-permute-start | bytes 208904 | tf_op jit(solution)/shard_map/ppermute | solution.py:236
  4.6 2.9 %collective-permute-start.2 = (bf16[272,128]{1,0:T(8,128)(2,1)}, bf16[272,128]{1,0:T(8,128)(2,1)S(1)}, u32[]{:S(2)}, u32[]{:S(2)}) collective-permute-start(bf16[272,128]{1,0:T(8,128)(2,1)} %get-tuple-element.16), channel_id=1, source_target_pairs={{0,9},{1,8},{2,11},{3,10},{4,13},{5,12},{6,15},{7,14},{8,17},{9,16... | collective-permute-start | bytes 208904 | tf_op jit(solution)/shard_map/ppermute | solution.py:236
  7.5 1.5 %collective-permute-start.3 = (bf16[272,128]{1,0:T(8,128)(2,1)}, bf16[272,128]{1,0:T(8,128)(2,1)S(1)}, u32[]{:S(2)}, u32[]{:S(2)}) collective-permute-start(bf16[272,128]{1,0:T(8,128)(2,1)} %get-tuple-element.17), channel_id=1, source_target_pairs={{0,16},{1,17},{2,18},{3,19},{4,20},{5,21},{6,22},{7,23},{8,24},{9,... | collective-permute-start | bytes 208904 | tf_op jit(solution)/shard_map/ppermute | solution.py:236
  9.0 1.5 %collective-permute-start.4 = (bf16[272,128]{1,0:T(8,128)(2,1)}, bf16[272,128]{1,0:T(8,128)(2,1)S(1)}, u32[]{:S(2)}, u32[]{:S(2)}) collective-permute-start(bf16[272,128]{1,0:T(8,128)(2,1)} %get-tuple-element.18), channel_id=1, source_target_pairs={{0,17},{1,16},{2,19},{3,18},{4,21},{5,20},{6,23},{7,22},{8,25},{9,... | collective-permute-start | bytes 208904 | tf_op jit(solution)/shard_map/ppermute | solution.py:236
  10.6 0.0 collective-permute-done.refs_1_
  10.6 1.7 %collective-permute-start.5 = (bf16[272,128]{1,0:T(8,128)(2,1)}, bf16[272,128]{1,0:T(8,128)(2,1)S(1)}, u32[]{:S(2)}, u32[]{:S(2)}) collective-permute-start(bf16[272,128]{1,0:T(8,128)(2,1)} %get-tuple-element.19), channel_id=1, source_target_pairs={{0,24},{1,25},{2,26},{3,27},{4,28},{5,29},{6,30},{7,31},{8,0},{9,1... | collective-permute-start | bytes 208904 | tf_op jit(solution)/shard_map/ppermute | solution.py:236
  12.2 0.0 collective-permute-done.1.refs_2_
  12.2 1.8 %collective-permute-start.6 = (bf16[272,128]{1,0:T(8,128)(2,1)}, bf16[272,128]{1,0:T(8,128)(2,1)S(1)}, u32[]{:S(2)}, u32[]{:S(2)}) collective-permute-start(bf16[272,128]{1,0:T(8,128)(2,1)} %get-tuple-element.20), channel_id=1, source_target_pairs={{0,25},{1,24},{2,27},{3,26},{4,29},{5,28},{6,31},{7,30},{8,1},{9,0... | collective-permute-start | bytes 208904 | tf_op jit(solution)/shard_map/ppermute | solution.py:236
  14.0 10.1 %all-to-all-start = ((bf16[32,32,128]{2,1,0:T(8,128)(2,1)}), bf16[32,32,128]{2,1,0:T(8,128)(2,1)S(1)}, u32[]{:S(2)}, u32[]{:S(2)}) async-start(bf16[32,32,128]{2,1,0:T(8,128)(2,1)} %get-tuple-element.21), calls=%async_computation | async-start | bytes 524288 | tf_op jit(solution)/shard_map/all_to_all | solution.py:258
  24.3 0.0 collective-permute-done.2.refs_3_
  24.3 0.0 collective-permute-done.3.refs_4_
  24.3 0.0 collective-permute-done.4.refs_5_
  24.3 0.0 collective-permute-done.5.refs_6_
  24.3 0.0 collective-permute-done.6.refs_7_
  24.3 0.9 %fusion = bf16[256,128]{1,0:T(8,128)(2,1)S(1)} fusion(bf16[272,128]{1,0:T(8,128)(2,1)S(1)} %collective-permute-done.6.refs_7_, bf16[272,128]{1,0:T(8,128)(2,1)S(1)} %collective-permute-done.5.refs_6_, bf16[272,128]{1,0:T(8,128)(2,1)S(1)} %collective-permute-done.4.refs_5_, bf16[272,128]{1,0:T(8,128)(2,1)S(1)} %collective-permute-done.3.refs_4_, ...), kind=kLoop, calls=%fused_computation.2 | loop fusion | flops 491520 | bytes 589832 | tf_op jit(solution)/shard_map/add | solution.py:261
  25.2 6.4 %collective-permute-start.9 = (bf16[256,128]{1,0:T(8,128)(2,1)S(1)}, bf16[256,128]{1,0:T(8,128)(2,1)S(1)}, u32[]{:S(2)}, u32[]{:S(2)}) collective-permute-start(bf16[256,128]{1,0:T(8,128)(2,1)S(1)} %fusion), channel_id=1, source_target_pairs={{0,5},{1,4},{8,13},{9,12},{16,21},{17,20},{24,29},{25,28},{32,37},... | collective-permute-start | bytes 196616 | tf_op jit(solution)/shard_map/ppermute | solution.py:231
  31.6 1.3 %collective-permute-start.8 = (bf16[256,128]{1,0:T(8,128)(2,1)S(1)}, bf16[256,128]{1,0:T(8,128)(2,1)S(1)}, u32[]{:S(2)}, u32[]{:S(2)}) collective-permute-start(bf16[256,128]{1,0:T(8,128)(2,1)S(1)} %fusion), channel_id=1, source_target_pairs={{0,6},{1,7},{8,14},{9,15},{16,22},{17,23},{24,30},{25,31},{32,38},... | collective-permute-start | bytes 196616 | tf_op jit(solution)/shard_map/ppermute | solution.py:231
  32.9 1.3 %collective-permute-start.7 = (bf16[256,128]{1,0:T(8,128)(2,1)S(1)}, bf16[256,128]{1,0:T(8,128)(2,1)S(1)}, u32[]{:S(2)}, u32[]{:S(2)}) collective-permute-start(bf16[256,128]{1,0:T(8,128)(2,1)S(1)} %fusion), channel_id=1, source_target_pairs={{0,2},{1,3},{8,10},{9,11},{16,18},{17,19},{24,26},{25,27},{32,34},... | collective-permute-start | bytes 196616 | tf_op jit(solution)/shard_map/ppermute | solution.py:231
  34.2 0.0 collective-permute-done.9
  34.2 1.1 %collective-permute-done.8 = bf16[256,128]{1,0:T(8,128)(2,1)S(1)} collective-permute-done((bf16[256,128]{1,0:T(8,128)(2,1)S(1)}, bf16[256,128]{1,0:T(8,128)(2,1)S(1)}, u32[]{:S(2)}, u32[]{:S(2)}) %collective-permute-start.8) | collective-permute-done | bytes 65568 | tf_op jit(solution)/shard_map/ppermute | solution.py:231
  35.4 1.2 %collective-permute-done.7 = bf16[256,128]{1,0:T(8,128)(2,1)S(1)} collective-permute-done((bf16[256,128]{1,0:T(8,128)(2,1)S(1)}, bf16[256,128]{1,0:T(8,128)(2,1)S(1)}, u32[]{:S(2)}, u32[]{:S(2)}) %collective-permute-start.7) | collective-permute-done | bytes 65568 | tf_op jit(solution)/shard_map/ppermute | solution.py:231
  36.6 0.0 copy-start
  36.6 0.7 %collective-permute-start.10 = (bf16[256,128]{1,0:T(8,128)(2,1)S(1)}, bf16[256,128]{1,0:T(8,128)(2,1)S(1)}, u32[]{:S(2)}, u32[]{:S(2)}) collective-permute-start(bf16[256,128]{1,0:T(8,128)(2,1)S(1)} %add_add_fusion), channel_id=1, source_target_pairs={{0,1},{1,0},{2,3},{3,2},{4,5},{5,4},{6,7},{7,6},{8,9},{9,8},{10,11... | collective-permute-start | bytes 196616 | tf_op jit(solution)/shard_map/ppermute | solution.py:236
  37.3 0.0 all-to-all-done.refs_8_
  37.3 0.0 copy-start.1
  37.3 0.9 %copy-done.1 = bf16[272,128]{1,0:T(8,128)(2,1)S(1)} copy-done((bf16[272,128]{1,0:T(8,128)(2,1)S(1)}, bf16[272,128]{1,0:T(8,128)(2,1)}, u32[]{:S(2)}) %copy-start.1) | copy-done | bytes 69656
  38.2 2.4 %shard_map.60 = f32[32,40,128]{2,1,0:T(8,128)S(1)} custom-call(s32[1]{0:T(128)} %bitcast.place_ref, bf16[272,128]{1,0:T(8,128)(2,1)S(1)} %copy-done.1, bf16[272,128]{1,0:T(8,128)(2,1)S(1)} %collective-permute-done.refs_1_, bf16[272,128]{1,0:T(8,128)(2,1)S(1)} %collective-permute-done.1.refs_2_, bf16[272,128]{1,0:T(8,128)(2,1)S(1)} %collective-permute-done.2.refs_3_, ...), custom_call_target="tpu_custom_call" | custom-call | flops 536870912 | bytes 2097152 | tf_op jit(solution)/shard_map/pallas_call | solution.py:267
  40.5 0.8 %convert_element_type.15 = f16[32,40,128]{2,1,0:T(8,128)(2,1)} convert(f32[32,40,128]{2,1,0:T(8,128)S(1)} %shard_map.60) | non-fusion elementwise | flops 163840 | bytes 983040 | tf_op jit(solution)/shard_map/convert_element_type | solution.py:275
  41.3 0.0 collective-permute-done.10
  41.4 2.8 %collective-permute-start.13 = (bf16[2,256,128]{2,1,0:T(8,128)(2,1)S(1)}, bf16[2,256,128]{2,1,0:T(8,128)(2,1)S(1)}, u32[]{:S(2)}, u32[]{:S(2)}) collective-permute-start(bf16[2,256,128]{2,1,0:T(8,128)(2,1)S(1)} %pad_maximum_fusion.a0_ref), channel_id=1, source_target_pairs={{0,24},{1,25},{2,26},{3,27},{4,28},{5,29},{6,30},{7,31},{8,0},{9,1... | collective-permute-start | bytes 393224 | tf_op jit(solution)/shard_map/ppermute | solution.py:236
  44.2 0.8 %collective-permute-start.12 = (bf16[2,256,128]{2,1,0:T(8,128)(2,1)S(1)}, bf16[2,256,128]{2,1,0:T(8,128)(2,1)S(1)}, u32[]{:S(2)}, u32[]{:S(2)}) collective-permute-start(bf16[2,256,128]{2,1,0:T(8,128)(2,1)S(1)} %pad_maximum_fusion.a0_ref), channel_id=1, source_target_pairs={{0,16},{1,17},{2,18},{3,19},{4,20},{5,21},{6,22},{7,23},{8,24},{9,... | collective-permute-start | bytes 393224 | tf_op jit(solution)/shard_map/ppermute | solution.py:236
  45.0 0.9 %collective-permute-start.11 = (bf16[2,256,128]{2,1,0:T(8,128)(2,1)S(1)}, bf16[2,256,128]{2,1,0:T(8,128)(2,1)S(1)}, u32[]{:S(2)}, u32[]{:S(2)}) collective-permute-start(bf16[2,256,128]{2,1,0:T(8,128)(2,1)S(1)} %pad_maximum_fusion.a0_ref), channel_id=1, source_target_pairs={{0,8},{1,9},{2,10},{3,11},{4,12},{5,13},{6,14},{7,15},{8,16},{9,17... | collective-permute-start | bytes 393224 | tf_op jit(solution)/shard_map/ppermute | solution.py:236
  45.8 8.2 %all-to-all-start.1 = ((f16[32,40,128]{2,1,0:T(8,128)(2,1)}), f16[32,40,128]{2,1,0:T(8,128)(2,1)S(1)}, u32[]{:S(2)}, u32[]{:S(2)}) async-start(f16[32,40,128]{2,1,0:T(8,128)(2,1)} %convert_element_type.15), calls=%async_computation.1 | async-start | bytes 655360 | tf_op jit(solution)/shard_map/all_to_all | solution.py:279
  54.0 0.0 collective-permute-done.13.a3_ref
  54.0 0.0 collective-permute-done.12.a2_ref
  54.0 0.0 collective-permute-done.11.a1_ref
  54.1 0.0 copy-done
  54.1 7.7 %shard_map.61 = bf16[128,8192]{1,0:T(8,128)(2,1)} custom-call(s32[1]{0:T(128)} %bitcast.place_ref, bf16[128,8192]{1,0:T(8,128)(2,1)} %q_hbm.3, bf16[2,128,1024]{2,1,0:T(8,128)(2,1)S(1)} %copy-done, bf16[2,256,128]{2,1,0:T(8,128)(2,1)S(1)} %pad_maximum_fusion.a0_ref, bf16[2,256,128]{2,1,0:T(8,128)(2,1)S(1)} %collective-permute-done.11.a1_ref, ...), custom_call_target="tpu_custom_call" | custom-call | flops 68719476736 | bytes 16777216 | tf_op jit(solution)/shard_map/pallas_call | solution.py:280
  61.8 4.0 %all-to-all-done.1 = f16[32,40,128]{2,1,0:T(8,128)(2,1)S(1)} async-done(((f16[32,40,128]{2,1,0:T(8,128)(2,1)}), f16[32,40,128]{2,1,0:T(8,128)(2,1)S(1)}, u32[]{:S(2)}, u32[]{:S(2)}) %all-to-all-start.1) | async-done | bytes 327712 | tf_op jit(solution)/shard_map/all_to_all | solution.py:279
  65.8 0.9 %shard_map.62 = bf16[4,8192]{1,0:T(4,128)(2,1)} custom-call(f32[32,40,128]{2,1,0:T(8,128)S(1)} %convert_element_type.16.in_ref), custom_call_target="tpu_custom_call" | custom-call | flops 1048576 | bytes 1048576 | tf_op jit(solution)/shard_map/pallas_call | solution.py:297
  (4 shorter events, 0.1 us)
Async XLA Ops:
  2.8 7.8 %collective-permute-start = (bf16[272,128]{1,0:T(8,128)(2,1)}, bf16[272,128]{1,0:T(8,128)(2,1)S(1)}, u32[]{:S(2)}, u32[]{:S(2)}) collective-permute-start(bf16[272,128]{1,0:T(8,128)(2,1)} %get-tuple-element.14), channel_id=1, source_target_pairs={{0,1},{1,0},{2,3},{3,2},{4,5},{5,4},{6,7},{7,6},{8,9},{9,8},{10,11... | collective-permute-start | bytes 208904 | tf_op jit(solution)/shard_map/ppermute | solution.py:236
  3.0 9.3 %collective-permute-start.1 = (bf16[272,128]{1,0:T(8,128)(2,1)}, bf16[272,128]{1,0:T(8,128)(2,1)S(1)}, u32[]{:S(2)}, u32[]{:S(2)}) collective-permute-start(bf16[272,128]{1,0:T(8,128)(2,1)} %get-tuple-element.15), channel_id=1, source_target_pairs={{0,8},{1,9},{2,10},{3,11},{4,12},{5,13},{6,14},{7,15},{8,16},{9,17... | collective-permute-start | bytes 208904 | tf_op jit(solution)/shard_map/ppermute | solution.py:236
  4.6 19.7 %collective-permute-start.2 = (bf16[272,128]{1,0:T(8,128)(2,1)}, bf16[272,128]{1,0:T(8,128)(2,1)S(1)}, u32[]{:S(2)}, u32[]{:S(2)}) collective-permute-start(bf16[272,128]{1,0:T(8,128)(2,1)} %get-tuple-element.16), channel_id=1, source_target_pairs={{0,9},{1,8},{2,11},{3,10},{4,13},{5,12},{6,15},{7,14},{8,17},{9,16... | collective-permute-start | bytes 208904 | tf_op jit(solution)/shard_map/ppermute | solution.py:236
  7.5 16.8 %collective-permute-start.3 = (bf16[272,128]{1,0:T(8,128)(2,1)}, bf16[272,128]{1,0:T(8,128)(2,1)S(1)}, u32[]{:S(2)}, u32[]{:S(2)}) collective-permute-start(bf16[272,128]{1,0:T(8,128)(2,1)} %get-tuple-element.17), channel_id=1, source_target_pairs={{0,16},{1,17},{2,18},{3,19},{4,20},{5,21},{6,22},{7,23},{8,24},{9,... | collective-permute-start | bytes 208904 | tf_op jit(solution)/shard_map/ppermute | solution.py:236
  9.0 15.3 %collective-permute-start.4 = (bf16[272,128]{1,0:T(8,128)(2,1)}, bf16[272,128]{1,0:T(8,128)(2,1)S(1)}, u32[]{:S(2)}, u32[]{:S(2)}) collective-permute-start(bf16[272,128]{1,0:T(8,128)(2,1)} %get-tuple-element.18), channel_id=1, source_target_pairs={{0,17},{1,16},{2,19},{3,18},{4,21},{5,20},{6,23},{7,22},{8,25},{9,... | collective-permute-start | bytes 208904 | tf_op jit(solution)/shard_map/ppermute | solution.py:236
  10.6 13.7 %collective-permute-start.5 = (bf16[272,128]{1,0:T(8,128)(2,1)}, bf16[272,128]{1,0:T(8,128)(2,1)S(1)}, u32[]{:S(2)}, u32[]{:S(2)}) collective-permute-start(bf16[272,128]{1,0:T(8,128)(2,1)} %get-tuple-element.19), channel_id=1, source_target_pairs={{0,24},{1,25},{2,26},{3,27},{4,28},{5,29},{6,30},{7,31},{8,0},{9,1... | collective-permute-start | bytes 208904 | tf_op jit(solution)/shard_map/ppermute | solution.py:236
  12.2 12.1 %collective-permute-start.6 = (bf16[272,128]{1,0:T(8,128)(2,1)}, bf16[272,128]{1,0:T(8,128)(2,1)S(1)}, u32[]{:S(2)}, u32[]{:S(2)}) collective-permute-start(bf16[272,128]{1,0:T(8,128)(2,1)} %get-tuple-element.20), channel_id=1, source_target_pairs={{0,25},{1,24},{2,27},{3,26},{4,29},{5,28},{6,31},{7,30},{8,1},{9,0... | collective-permute-start | bytes 208904 | tf_op jit(solution)/shard_map/ppermute | solution.py:236
  14.0 23.2 %all-to-all-start = ((bf16[32,32,128]{2,1,0:T(8,128)(2,1)}), bf16[32,32,128]{2,1,0:T(8,128)(2,1)S(1)}, u32[]{:S(2)}, u32[]{:S(2)}) async-start(bf16[32,32,128]{2,1,0:T(8,128)(2,1)} %get-tuple-element.21), calls=%async_computation | async-start | bytes 524288 | tf_op jit(solution)/shard_map/all_to_all | solution.py:258
  25.2 9.0 %collective-permute-start.9 = (bf16[256,128]{1,0:T(8,128)(2,1)S(1)}, bf16[256,128]{1,0:T(8,128)(2,1)S(1)}, u32[]{:S(2)}, u32[]{:S(2)}) collective-permute-start(bf16[256,128]{1,0:T(8,128)(2,1)S(1)} %fusion), channel_id=1, source_target_pairs={{0,5},{1,4},{8,13},{9,12},{16,21},{17,20},{24,29},{25,28},{32,37},... | collective-permute-start | bytes 196616 | tf_op jit(solution)/shard_map/ppermute | solution.py:231
  31.6 3.7 %collective-permute-start.8 = (bf16[256,128]{1,0:T(8,128)(2,1)S(1)}, bf16[256,128]{1,0:T(8,128)(2,1)S(1)}, u32[]{:S(2)}, u32[]{:S(2)}) collective-permute-start(bf16[256,128]{1,0:T(8,128)(2,1)S(1)} %fusion), channel_id=1, source_target_pairs={{0,6},{1,7},{8,14},{9,15},{16,22},{17,23},{24,30},{25,31},{32,38},... | collective-permute-start | bytes 196616 | tf_op jit(solution)/shard_map/ppermute | solution.py:231
  32.9 3.6 %collective-permute-start.7 = (bf16[256,128]{1,0:T(8,128)(2,1)S(1)}, bf16[256,128]{1,0:T(8,128)(2,1)S(1)}, u32[]{:S(2)}, u32[]{:S(2)}) collective-permute-start(bf16[256,128]{1,0:T(8,128)(2,1)S(1)} %fusion), channel_id=1, source_target_pairs={{0,2},{1,3},{8,10},{9,11},{16,18},{17,19},{24,26},{25,27},{32,34},... | collective-permute-start | bytes 196616 | tf_op jit(solution)/shard_map/ppermute | solution.py:231
  36.6 17.5 %copy-start = (bf16[2,128,1024]{2,1,0:T(8,128)(2,1)S(1)}, bf16[2,128,1024]{2,1,0:T(8,128)(2,1)}, u32[]{:S(2)}) copy-start(bf16[2,128,1024]{2,1,0:T(8,128)(2,1)} %kv_hbm.3) | copy-start | bytes 1572868
  36.6 4.7 %collective-permute-start.10 = (bf16[256,128]{1,0:T(8,128)(2,1)S(1)}, bf16[256,128]{1,0:T(8,128)(2,1)S(1)}, u32[]{:S(2)}, u32[]{:S(2)}) collective-permute-start(bf16[256,128]{1,0:T(8,128)(2,1)S(1)} %add_add_fusion), channel_id=1, source_target_pairs={{0,1},{1,0},{2,3},{3,2},{4,5},{5,4},{6,7},{7,6},{8,9},{9,8},{10,11... | collective-permute-start | bytes 196616 | tf_op jit(solution)/shard_map/ppermute | solution.py:236
  37.3 0.9 %copy-start.1 = (bf16[272,128]{1,0:T(8,128)(2,1)S(1)}, bf16[272,128]{1,0:T(8,128)(2,1)}, u32[]{:S(2)}) copy-start(bf16[272,128]{1,0:T(8,128)(2,1)} %get-tuple-element.13.refs_0_) | copy-start | bytes 208900
  41.4 12.7 %collective-permute-start.13 = (bf16[2,256,128]{2,1,0:T(8,128)(2,1)S(1)}, bf16[2,256,128]{2,1,0:T(8,128)(2,1)S(1)}, u32[]{:S(2)}, u32[]{:S(2)}) collective-permute-start(bf16[2,256,128]{2,1,0:T(8,128)(2,1)S(1)} %pad_maximum_fusion.a0_ref), channel_id=1, source_target_pairs={{0,24},{1,25},{2,26},{3,27},{4,28},{5,29},{6,30},{7,31},{8,0},{9,1... | collective-permute-start | bytes 393224 | tf_op jit(solution)/shard_map/ppermute | solution.py:236
  44.2 9.9 %collective-permute-start.12 = (bf16[2,256,128]{2,1,0:T(8,128)(2,1)S(1)}, bf16[2,256,128]{2,1,0:T(8,128)(2,1)S(1)}, u32[]{:S(2)}, u32[]{:S(2)}) collective-permute-start(bf16[2,256,128]{2,1,0:T(8,128)(2,1)S(1)} %pad_maximum_fusion.a0_ref), channel_id=1, source_target_pairs={{0,16},{1,17},{2,18},{3,19},{4,20},{5,21},{6,22},{7,23},{8,24},{9,... | collective-permute-start | bytes 393224 | tf_op jit(solution)/shard_map/ppermute | solution.py:236
  45.0 9.1 %collective-permute-start.11 = (bf16[2,256,128]{2,1,0:T(8,128)(2,1)S(1)}, bf16[2,256,128]{2,1,0:T(8,128)(2,1)S(1)}, u32[]{:S(2)}, u32[]{:S(2)}) collective-permute-start(bf16[2,256,128]{2,1,0:T(8,128)(2,1)S(1)} %pad_maximum_fusion.a0_ref), channel_id=1, source_target_pairs={{0,8},{1,9},{2,10},{3,11},{4,12},{5,13},{6,14},{7,15},{8,16},{9,17... | collective-permute-start | bytes 393224 | tf_op jit(solution)/shard_map/ppermute | solution.py:236
  45.8 19.9 %all-to-all-start.1 = ((f16[32,40,128]{2,1,0:T(8,128)(2,1)}), f16[32,40,128]{2,1,0:T(8,128)(2,1)S(1)}, u32[]{:S(2)}, u32[]{:S(2)}) async-start(f16[32,40,128]{2,1,0:T(8,128)(2,1)} %convert_element_type.15), calls=%async_computation.1 | async-start | bytes 655360 | tf_op jit(solution)/shard_map/all_to_all | solution.py:279
